TPU v7x, 128 devices: a whole 4x4x4 slice. The times are simulated.
128 devices in a mesh: blk: 32 (over x, y, z_hi), ha: 4 (over z_lo, core).
Axes of the slice: x: 4, y: 4, z: 4 (z_hi: 2, z_lo: 2; z = z_hi * 2 + z_lo), core: 2. Of those that a mesh axis runs over, the one named last changes fastest.
Arguments:
- int_temp: float32 [32, 1024, 1024], P(None, 'blk', 'ha'), may hold values from 0.5 to 3
- int_degree: float32 [32, 1024, 1024], P(None, 'blk', 'ha'), may hold values from 0.05 to 0.6
- int_affinity: float32 [32, 1024, 1024], P(None, 'blk', 'ha'), may hold values from 0.02 to 0.15
- skin_humidity: float32 [16, 256, 8192], P(None, 'ha', 'blk'), may hold values from 0.6 to 1
- skin_temp: float32 [16, 256, 8192], P(None, 'ha', 'blk'), may hold values from 0 to 2
- skin_degree: float32 [16, 256, 8192], P(None, 'ha', 'blk'), may hold values from 0.05 to 0.6
- ambient: float32 [256, 8192], P('ha', 'blk'), may hold values from 0.4 to 0.8
- colmap: int32 [8192], P('blk'), may hold values from 0 to 16383, as said below
Outputs:
- int_temp_out: float32 [32, 1024, 1024], P(None, 'blk', 'ha')
- int_degree_out: float32 [32, 1024, 1024], P(None, 'blk', 'ha')
- skin_humidity_out: float32 [16, 256, 8192], P(None, 'ha', 'blk')
- skin_temp_out: float32 [16, 256, 8192], P(None, 'ha', 'blk')
Inputs may be any that keep to these rules, and one draw needn't show every extreme that they name: `colmap`: coarse column c belongs to device c // 128 of blk+ha. Among the 256 arcs of one device at most 4 name columns of any one device, and in every draw one device has exactly 4 arcs of every device's arcs naming its columns.
All inputs are finite; a program needn't handle non-finite values.
Results may differ from a plain program's by a relative error of at most 0.00009.
Values sent between devices are 32-bit elements; how exact they have to be, the bound alone decides.
A program may use at most 128 MiB of HBM per device.

v0:
```python
import jax
import jax.numpy as jnp
from jax import lax
from jax.sharding import PartitionSpec as P

CB = 8
INT_STEPS = 2
SUB = 4


def with_halo(block, sides, width, periodic):
    for axis, dim in sides:
        count = lax.axis_size(axis)
        forward = [(i, i + 1) for i in range(count - 1)]
        if periodic:
            forward.append((count - 1, 0))
        backward = [(target, source) for source, target in forward]
        low = lax.ppermute(
            lax.slice_in_dim(block, block.shape[dim] - width, None, axis=dim), axis, forward
        )
        high = lax.ppermute(lax.slice_in_dim(block, 0, width, axis=dim), axis, backward)
        block = jnp.concatenate([low, block, high], axis=dim)
    return block


def arrhenius(field, energy):
    return jnp.exp(energy * (1.0 / 293.15 - 1.0 / (293.15 + 10.0 * field)))


def neighbour_views(padded):
    return [
        padded[2:, 1:-1, 1:-1],
        padded[:-2, 1:-1, 1:-1],
        padded[1:-1, 2:, 1:-1],
        padded[1:-1, :-2, 1:-1],
        padded[1:-1, 1:-1, 2:],
        padded[1:-1, 1:-1, :-2],
    ]


def interior_update(padded, thermal, degree, affinity):
    views = neighbour_views(padded)
    laplace = views[0] + views[1] + views[2] + views[3] + views[4] + views[5] - 6.0 * thermal
    hydration = affinity * (0.85 - degree) * arrhenius(thermal, 4000.0)
    return (thermal + 0.15 * laplace + 4.0 * hydration, degree + hydration)


def skin_step(hum_pad, temp_pad, degree, bound_temp, ambient):
    inner_hum = jnp.ones((1,) + hum_pad.shape[1:], jnp.float32)
    outer_hum = jnp.pad(ambient, 1)[None]
    hum_full = jnp.concatenate([inner_hum, hum_pad, outer_hum], axis=0)
    temp_full = jnp.concatenate([jnp.pad(bound_temp, 1)[None], temp_pad, temp_pad[-1:]], axis=0)
    diffusion = (
        0.07 * (0.05 + 0.95 / (1.0 + ((1.0 - hum_full) / 0.25) ** 8)) * arrhenius(temp_full, 2700.0)
    )
    hum_mid = hum_full[1:-1, 1:-1, 1:-1]
    temp_mid = temp_full[1:-1, 1:-1, 1:-1]
    diff_mid = diffusion[1:-1, 1:-1, 1:-1]
    moisture = jnp.zeros_like(hum_mid)
    conduction = jnp.zeros_like(temp_mid)
    for hum_view, temp_view, diff_view in zip(
        neighbour_views(hum_full), neighbour_views(temp_full), neighbour_views(diffusion)
    ):
        moisture = moisture + 0.5 * (diff_mid + diff_view) * (hum_view - hum_mid)
        conduction = conduction + (temp_view - temp_mid)
    hydration = (
        0.08 * (0.85 - degree) * arrhenius(temp_mid, 4000.0) / (1.0 + (7.5 - 7.5 * hum_mid) ** 4)
    )
    evaporation = 0.5 * (diff_mid[-1] + diffusion[-1, 1:-1, 1:-1]) * (hum_mid[-1] - ambient)
    hum_new = hum_mid + moisture - 0.3 * hydration
    temp_new = temp_mid + 0.15 * conduction + 4.0 * hydration
    temp_new = temp_new.at[-1].add(-2.0 * evaporation)
    inflow = 0.15 * (bound_temp - temp_mid[0])
    return (hum_new, temp_new, degree + hydration, inflow)


def on_device(
    int_temp, int_degree, int_affinity, skin_humidity, skin_temp, skin_degree, ambient, colmap
):
    blk_index = lax.axis_index("blk")
    blk_count = lax.axis_size("blk")
    ha_index = lax.axis_index("ha")
    ha_count = lax.axis_size("ha")
    devices = blk_count * ha_count
    layers_all, cells_x, cells_y = int_temp.shape
    layers = layers_all // ha_count
    rows, arcs = (skin_humidity.shape[1], skin_humidity.shape[2])
    cols_dev = cells_x // CB * (cells_y // CB)
    thermal, degree = (int_temp, int_degree)
    for stepno in range(INT_STEPS):
        plan_widened = with_halo(thermal, (("blk", 1), ("ha", 2)), 1, False)
        plan_widened = plan_widened.at[:, 0, :].set(
            jnp.where(blk_index == 0, plan_widened[:, 1, :], plan_widened[:, 0, :])
        )
        plan_widened = plan_widened.at[:, -1, :].set(
            jnp.where(blk_index == blk_count - 1, plan_widened[:, -2, :], plan_widened[:, -1, :])
        )
        plan_widened = plan_widened.at[:, :, 0].set(
            jnp.where(ha_index == 0, plan_widened[:, :, 1], plan_widened[:, :, 0])
        )
        plan_widened = plan_widened.at[:, :, -1].set(
            jnp.where(ha_index == ha_count - 1, plan_widened[:, :, -2], plan_widened[:, :, -1])
        )
        thermal, degree = interior_update(
            jnp.pad(plan_widened, ((1, 1), (0, 0), (0, 0)), mode="edge"),
            thermal,
            degree,
            int_affinity,
        )
    column_temp = (
        thermal.reshape(layers_all, cells_x // CB, CB, cells_y // CB, CB)
        .mean(axis=(2, 4))
        .reshape(layers_all, cols_dev)
    )
    table = lax.all_gather(column_temp, ("blk", "ha"), axis=1, tiled=True)
    band_rows = lax.dynamic_slice_in_dim(table, ha_index * layers, layers, 0)
    bound_layers = jnp.take(band_rows, colmap, axis=1)
    bound = jnp.repeat(bound_layers, rows // layers, axis=0)
    hum, temp, sdeg = (skin_humidity, skin_temp, skin_degree)
    total = jnp.zeros((rows, arcs), jnp.float32)
    for substep in range(SUB):
        fields = jnp.stack([hum, temp])
        widened = with_halo(fields, (("blk", 3), ("ha", 2)), 1, True)
        widened = widened.at[:, :, 0, :].set(
            jnp.where(ha_index == 0, widened[:, :, 1, :], widened[:, :, 0, :])
        )
        widened = widened.at[:, :, -1, :].set(
            jnp.where(ha_index == ha_count - 1, widened[:, :, -2, :], widened[:, :, -1, :])
        )
        hum_pad = widened[0]
        temp_pad = widened[1]
        hum, temp, sdeg, inflow = skin_step(hum_pad, temp_pad, sdeg, bound, ambient)
        total = total + inflow
    heat_layers = total.reshape(layers, rows // layers, arcs).sum(axis=1)
    flux_dense = jnp.zeros((layers, devices * cols_dev), jnp.float32).at[:, colmap].add(heat_layers)
    flux_rows = jnp.zeros((layers_all, devices * cols_dev), jnp.float32)
    flux_rows = lax.dynamic_update_slice_in_dim(flux_rows, flux_dense, ha_index * layers, 0)
    uptake = lax.psum_scatter(flux_rows, ("blk", "ha"), scatter_dimension=1, tiled=True)
    cell_uptake = uptake.reshape(layers_all, cells_x // CB, cells_y // CB)
    cell_uptake = jnp.repeat(jnp.repeat(cell_uptake, CB, axis=1), CB, axis=2)
    thermal_out = thermal - 0.5 * cell_uptake / (CB * CB)
    return (thermal_out, degree, hum, temp)


def solution(mesh):
    return jax.shard_map(
        on_device,
        mesh=mesh,
        in_specs=(
            P(None, "blk", "ha"),
            P(None, "blk", "ha"),
            P(None, "blk", "ha"),
            P(None, "ha", "blk"),
            P(None, "ha", "blk"),
            P(None, "ha", "blk"),
            P("ha", "blk"),
            P("blk"),
        ),
        out_specs=(
            P(None, "blk", "ha"),
            P(None, "blk", "ha"),
            P(None, "ha", "blk"),
            P(None, "ha", "blk"),
        ),
        check_vma=False,
    )
```

profile of v0, /device:TPU:1, one launch (start us, length us, event | category | flops | bytes accessed | tf_op | source)
XLA Modules:
  0.0 1002.0 jit_solution(4403895036692498598)
XLA Ops:
  8.3 6.3 collective-permute-start
  15.9 4.9 collective-permute-done.1
  22.7 4.6 collective-permute-start.2
  41.3 3.9 scatter.56
  46.3 6.2 scatter.59
  52.6 5.0 add_add_fusion
  57.6 4.7 collective-permute-start.4
  63.6 4.9 collective-permute-done.5
  86.2 3.9 scatter.64
  91.2 6.2 scatter.65
  97.5 5.0 fusion.204
  102.5 3.7 copy.295
  112.7 3.4 collective-permute-start.8
  116.5 3.9 collective-permute-start.9
  126.6 3.8 collective-permute-done.11
  130.4 4.5 pad_maximum_fusion.8
  143.7 39.4 %all-gather.2.cloned.1.call-done = f32[32,16384]{0,1:T(8,128)} async-done(((f32[32,128]{0,1:T(8,128)}), f32[32,16384]{0,1:T(8,128)}) %all-gather.2.cloned.1.call-update) | async-done | bytes 2097168 | tf_op jit(solution)/shard_map/all_gather | solution.py:115
  183.1 6.7 constant_dynamic-slice_fusion
  189.7 4.7 gather_fusion
  200.4 4.3 fusion.79
  213.7 6.1 collective-permute-start.13
  230.3 3.2 pad_maximum_fusion.9
  243.6 4.5 fusion.89
  258.0 7.3 collective-permute-start.17
  291.4 4.5 fusion.99
  304.8 7.7 collective-permute-start.21
  324.6 3.3 pad_maximum_fusion.11
  333.5 3.5 slice_bitcast_fusion
  338.3 5.4 scatter_custom_fusion
  343.7 5.9 copy.314
  360.6 4.8 fusion.108
  365.4 621.9 %reduce-scatter.2.cloned.1.call-done = f32[32,128]{1,0:T(8,128)} async-done(((f32[32,16384]{1,0:T(8,128)}), f32[32,128]{1,0:T(8,128)}) %reduce-scatter.2.cloned.1.call-update) | async-done | bytes 16400 | tf_op jit(solution)/shard_map/reduce_scatter | solution.py:138
  (273 shorter events, 178.4 us)
Async XLA Ops:
  7.2 175.9 %all-gather.2.cloned.1.call-start = ((), (), s32[]{:S(2)}) async-start(), calls=%async_computation.1 | async-start | bytes 8454144 | tf_op jit(solution)/shard_map/all_gather | solution.py:115
  8.3 7.6 collective-permute-start
  14.6 6.2 collective-permute-start.1
  22.4 11.5 %copy-start.20 = (f32[32,32,256]{2,1,0:T(8,128)S(1)}, f32[32,32,256]{2,1,0:T(8,128)}, u32[]{:S(2)}) copy-start(f32[32,32,256]{2,1,0:T(8,128)} %param.48) | copy-start | bytes 3145732
  22.7 6.9 collective-permute-start.2
  27.7 5.0 collective-permute-start.3
  57.6 11.3 %copy-start.21 = (f32[32,32,256]{2,1,0:T(8,128)}, f32[32,32,256]{2,1,0:T(8,128)S(1)}, u32[]{:S(2)}) copy-start(f32[32,32,256]{2,1,0:T(8,128)S(1)} %get-tuple-element.271) | copy-start | bytes 3145732
  57.6 6.0 collective-permute-start.4
  62.3 6.2 collective-permute-start.5
  69.2 5.2 collective-permute-start.6
  72.3 5.0 collective-permute-start.7
  109.7 877.6 %reduce-scatter.2.cloned.1.call-start = ((), (), s32[]{:S(2)}) async-start(), calls=%async_computation.2 | async-start | bytes 2113536 | tf_op jit(solution)/shard_map/reduce_scatter | solution.py:138
  111.1 9.3 copy-start.58
  112.7 8.4 collective-permute-start.8
  116.5 5.1 collective-permute-start.9
  123.1 2.4 collective-permute-start.10
  125.8 4.6 collective-permute-start.11
  126.6 162.9 %copy-start.55 = (f32[18]{0:T(128)}, f32[18]{0:T(128)S(1)}, u32[]{:S(2)}) copy-start(f32[18]{0:T(128)S(1)} %pad.140.clone) | copy-start | bytes 220
  209.2 13.3 %copy-start.5 = (f32[1,16,64,256]{3,2,1,0:T(8,128)S(1)}, f32[1,16,64,256]{3,2,1,0:T(8,128)}, u32[]{:S(2)}) copy-start(f32[1,16,64,256]{3,2,1,0:T(8,128)} %copy-done.4) | copy-start | bytes 3145732
  210.9 8.9 collective-permute-start.12
  213.7 7.5 collective-permute-start.13
  224.0 1.8 collective-permute-start.14
  226.0 4.4 collective-permute-start.15
  254.8 10.5 %collective-permute-start.16 = (f32[2,16,64,1]{2,1,3,0:T(8,128)}, f32[2,16,64,1]{2,1,3,0:T(8,128)}, u32[]{:S(2)}, u32[]{:S(2)}) collective-permute-start(f32[2,16,64,1]{2,1,3,0:T(8,128)} %copy.305), channel_id=1, source_target_pairs={{0,4},{4,8},{8,12},{12,16},{16,20},{20,24},{24,28},{28,32},{32,36}... | collective-permute-start | bytes 24584 | tf_op jit(solution)/shard_map/ppermute | solution.py:18
  258.0 9.4 collective-permute-start.17
  271.0 1.3 collective-permute-start.18
  273.1 4.3 collective-permute-start.19
  288.5 7.4 copy-start.1
  302.6 9.9 collective-permute-start.20
  304.8 9.8 collective-permute-start.21
  318.1 1.3 collective-permute-start.22
  320.3 4.3 collective-permute-start.23
  (53 other events, 142.4 us)
Sparse Core Ops, SparseCore 0:
  109.8 73.2 all-gather.1
  353.2 634.0 reduce-scatter.1
where the time goes:
time: 1020 us; the launch traced here: 1000 us
  waiting for transfers between devices  689 us (68%)
  local copies, waits for them, and re-layouts  127 us (12%)
  other arithmetic  104 us (10%)
  starting transfers between devices  66.7 us (7%)
  between operations  15.6 us (2%)
    reduce_scatter x1, waiting for transfers between devices, on_device(): lax.psum_scatter(flux_rows, ('blk', 'ha'), scatter_dimension=1, tiled=True)  622 us
    ppermute x12, starting transfers between devices, with_halo(): lax.ppermute(lax.slice_in_dim(block, 0, width, axis=dim), axis, backward)  40.6 us
    all_gather x1, waiting for transfers between devices, on_device(): table = lax.all_gather(column_temp, ('blk', 'ha'), axis=1, tiled=True)  39.4 us
    ppermute x12, starting transfers between devices, with_halo(): lax.ppermute(lax.slice_in_dim(block, block.shape[dim] - width, None, axis...  26.1 us
    ppermute x12, waiting for transfers between devices, with_halo(): lax.ppermute(lax.slice_in_dim(block, 0, width, axis=dim), axis, backward)  21.9 us
    concatenate x8, other arithmetic, with_halo(): block = jnp.concatenate([low, block, high], axis=dim)  20.6 us
  transfers between devices with their start and end apart: 26, of which 15 were waited for; matrix products, arithmetic and copies ran while one was open for 4% of the time, Pallas kernels for 0%

commit v1 on v0

v1 whole, which is shorter than its diff:
```python
import math

import jax
import jax.numpy as jnp
from jax import lax
from jax.experimental import pallas as pl
from jax.experimental.pallas import tpu as pltpu
from jax.sharding import PartitionSpec as P

F32 = jnp.float32
BF16 = jnp.bfloat16
MESH = pl.DeviceIdType.MESH

NZ, IX, IY = 32, 32, 256
DEPTH, ROWS, ARCS = 16, 64, 256
NB, NH = 32, 4
XC, RC = IX // 8, ROWS // 8
LN = 128

C27 = 2700.0 / 293.15 * math.log2(math.e)
C40 = 4000.0 / 293.15 * math.log2(math.e)

BULK = (0, 1, 2, 3)
WEDGE = (None, 4, 5, 6)
N_EX = 7


def rcp(x):
    r = pl.reciprocal(x, approx=True)
    return r * (2.0 - x * r)


def half_diff(h, t):
    s = 1.0 - h
    s2 = s * s
    s4 = s2 * s2
    q = t * rcp(29.315 + t)
    return (0.00175 + 0.03325 * rcp(1.0 + 65536.0 * (s4 * s4))) * jnp.exp2(C27 * q)


def rates(h, t):
    s = 1.0 - h
    s2 = s * s
    s4 = s2 * s2
    q = t * rcp(29.315 + t)
    d = (0.00175 + 0.03325 * rcp(1.0 + 65536.0 * (s4 * s4))) * jnp.exp2(C27 * q)
    g = 0.08 * rcp(1.0 + 3164.0625 * s4) * jnp.exp2(C40 * q)
    return d, g


def split3(a):
    a1 = a.astype(BF16).astype(F32)
    r1 = a - a1
    a2 = r1.astype(BF16).astype(F32)
    a3 = r1 - a2
    return jnp.concatenate([a1, a2, a3], axis=0).astype(BF16)


def pick(a, b, transpose_b=False):
    rows = a.shape[0]
    dims = (((1,), (1 if transpose_b else 0,)), ((), ()))
    out = lax.dot_general(split3(a), b, dims, preferred_element_type=F32)
    return out[:rows] + out[rows : 2 * rows] + out[2 * rows :]


def body(
    temp_in, deg_in, aff_in, hum_in, stemp_in, sdeg_in, amb_ref, col_ref,
    temp_out, deg_out, hum_out, stemp_out,
    th0, th1, al, af, hb0, hb1, tb0, tb1, db0, db1, gb, ab,
    cs, cr, rs, rr, ph, pd, dr, ics, icr, irs, irr,
    qs, qr, oh, o2, csum, csend, abuf, ws, rbuf, bnd, ub, vs, vr, ss, ubuf, ge,
    in_sem, out_sem, hs_send, hs_recv, q_send, q_recv, x1_send, x1_recv,
    x2_send, x2_recv, u2_send, u2_recv, u1_send, u1_recv,
):
    b = lax.axis_index("blk")
    ha = lax.axis_index("ha")
    lane = lax.broadcasted_iota(jnp.int32, (8, LN), 1)
    first = lane == 0
    final = lane == LN - 1
    lo, hi = slice(0, LN), slice(LN, 2 * LN)

    layers = pl.ds(1, NZ)
    slabs = pl.ds(1, DEPTH)
    xin = pl.ds(8, IX)
    rin = pl.ds(8, ROWS)
    loads = [
        pltpu.make_async_copy(src, dst, in_sem.at[i])
        for i, (src, dst) in enumerate(
            [
                (temp_in, th0.at[layers, xin, :]),
                (hum_in, hb0.at[slabs, rin, :]),
                (stemp_in, tb0.at[slabs, rin, :]),
                (aff_in, af),
                (deg_in, al),
                (sdeg_in, ab),
            ]
        )
    ]
    for copy in loads:
        copy.start()

    barrier = pltpu.get_barrier_semaphore()

    def greet(k, c):
        pl.semaphore_signal(barrier, inc=1, device_id=(lax.rem(b + k, NB), ha), device_id_type=MESH)
        return c

    lax.fori_loop(1, NB, greet, 0)
    for k in range(1, NH):
        pl.semaphore_signal(barrier, inc=1, device_id=(b, lax.rem(ha + k, NH)), device_id_type=MESH)

    col = col_ref[...]
    owner = col >> 7
    colf = jnp.broadcast_to(owner.astype(F32), (ARCS, ARCS))
    owner_down = colf.T
    q_i = lax.broadcasted_iota(jnp.int32, (ARCS, ARCS), 0)
    p_i = lax.broadcasted_iota(jnp.int32, (ARCS, ARCS), 1)
    earlier = jnp.where((owner_down == colf) & (q_i < p_i), 1.0, 0.0)
    rank = jnp.sum(earlier, axis=0, keepdims=True).astype(jnp.int32)
    ob = col >> 9
    pos = (ob >> 3) * LN + (((ob + b) & 7) << 4) + ((owner & 3) << 2) + rank
    posf = pos.astype(F32)
    pos_down = jnp.broadcast_to(posf, (LN, ARCS)).T
    val_down = jnp.broadcast_to((col & 511).astype(F32) + 1.0, (LN, ARCS)).T
    lanes_a = lax.broadcasted_iota(jnp.int32, (ARCS, LN), 1).astype(F32)
    for t in range(4):
        hit = jnp.where(pos_down == lanes_a + float(t * LN), val_down, 0.0)
        qs[t] = jnp.broadcast_to(jnp.sum(hit, axis=0, keepdims=True) - 1.0, (8, LN))
    slot_i = lax.broadcasted_iota(jnp.int32, (4 * LN, ARCS), 0).astype(F32)
    o2[...] = jnp.where(slot_i == posf, 1.0, 0.0).astype(BF16)

    zero = jnp.zeros((8, LN), F32)

    def clear(e, c):
        for side in range(2):
            for r in range(RC):
                cs[e, side, 8 * r : 8 * r + 8, :] = zero
            for f in range(2):
                rs[e, side, f] = jnp.zeros((DEPTH, ARCS), F32)
        return c

    lax.fori_loop(0, N_EX, clear, 0)
    for e in range(2):
        for side in range(2):
            ics[e, side] = jnp.zeros((IX, LN), F32)

    pl.semaphore_wait(barrier, NB - 1 + NH - 1)

    def to_blk(src, dst, send, recv):
        def go(k, c):
            to = lax.rem(b + k, NB)
            pltpu.make_async_remote_copy(
                src_ref=src.at[to // 8], dst_ref=dst.at[b], send_sem=send.at[to],
                recv_sem=recv.at[b], device_id=(to, ha), device_id_type=MESH,
            ).start()
            return c

        lax.fori_loop(1, NB, go, 0)

    def from_blk(src, dst, send, recv):
        def go(k, c):
            other = lax.rem(b + k, NB)
            copy = pltpu.make_async_remote_copy(
                src_ref=src.at[other // 8], dst_ref=dst.at[other], send_sem=send.at[other],
                recv_sem=recv.at[other], device_id=(other, ha), device_id_type=MESH,
            )
            copy.wait_send()
            copy.wait_recv()
            return c

        lax.fori_loop(1, NB, go, 0)
        dst[b] = src[b // 8]

    def combine(buf):
        tiles = []
        for t in range(4):
            acc = zero
            for j in range(8):
                acc = jnp.where((lane >> 4) == ((b + j) & 7), buf[t * 8 + j], acc)
            tiles.append(acc)
        return tiles

    def to_ha(src, dst, send, recv):
        for k in range(1, NH):
            to = lax.rem(ha + k, NH)
            pltpu.make_async_remote_copy(
                src_ref=src.at[to], dst_ref=dst.at[ha], send_sem=send.at[to],
                recv_sem=recv.at[ha], device_id=(b, to), device_id_type=MESH,
            ).start()

    def from_ha(src, dst, send, recv):
        for k in range(1, NH):
            other = lax.rem(ha + k, NH)
            copy = pltpu.make_async_remote_copy(
                src_ref=src.at[other], dst_ref=dst.at[other], send_sem=send.at[other],
                recv_sem=recv.at[other], device_id=(b, other), device_id_type=MESH,
            )
            copy.wait_send()
            copy.wait_recv()
        dst[ha] = src[ha]

    b_dn, b_up = lax.rem(b + NB - 1, NB), lax.rem(b + 1, NB)
    h_dn, h_up = lax.rem(ha + NH - 1, NH), lax.rem(ha + 1, NH)

    def halo(e, src_blk, dst_blk, src_ha, dst_ha):
        return [
            pltpu.make_async_remote_copy(
                src_ref=src.at[side], dst_ref=dst.at[1 - side],
                send_sem=hs_send.at[e, i], recv_sem=hs_recv.at[e, i],
                device_id=dev, device_id_type=MESH,
            )
            for i, (src, dst, side, dev) in enumerate(
                [
                    (src_blk, dst_blk, 0, (b_dn, ha)),
                    (src_blk, dst_blk, 1, (b_up, ha)),
                    (src_ha, dst_ha, 0, (b, h_dn)),
                    (src_ha, dst_ha, 1, (b, h_up)),
                ]
            )
        ]

    def skin_halo(e):
        return halo(e, cs.at[e], cr.at[e], rs.at[e], rr.at[e])

    def int_halo(e):
        return halo(N_EX + e, irs.at[e], irr.at[e], ics.at[e], icr.at[e])

    def start(copies):
        for copy in copies:
            copy.start()

    def wait(copies):
        for copy in copies:
            copy.wait()

    sub = lax.broadcasted_iota(jnp.int32, (8, LN), 0)

    def put_row(ref, m, row, half):
        tile = pl.ds(pl.multiple_of(((m - 1) // 8) * 8, 8), 8)
        here = sub == lax.rem(m - 1, 8)
        ref[tile, half] = jnp.where(here, jnp.broadcast_to(row, (8, LN)), ref[tile, half])

    def int_pack(e, m, r, x0, x1):
        rows = slice(8 * r, 8 * r + 8)
        ics[e, 0, rows, :] = jnp.where(lane == m, pltpu.roll(x0, m, 1), ics[e, 0, rows, :])
        ics[e, 1, rows, :] = jnp.where(lane == m, pltpu.roll(x1, m + 1, 1), ics[e, 1, rows, :])
        for side, at, k in ((0, 0, 0), (1, XC - 1, 7)):
            if r == at:
                for x, half in ((x0, lo), (x1, hi)):
                    put_row(irs.at[e, side], m, x[k : k + 1], half)

    def int_place(e, th):
        @pl.when(b == 0)
        def _():
            irr[e, 0] = irs[e, 0]

        @pl.when(b == NB - 1)
        def _():
            irr[e, 1] = irs[e, 1]

        @pl.when(ha == 0)
        def _():
            icr[e, 0] = ics[e, 0]

        @pl.when(ha == NH - 1)
        def _():
            icr[e, 1] = ics[e, 1]

        def go(m, c):
            th[m, 7:8, :] = irr[e, 0, pl.ds(m - 1, 1), :]
            th[m, 8 + IX : 9 + IX, :] = irr[e, 1, pl.ds(m - 1, 1), :]
            return c

        lax.fori_loop(1, NZ + 1, go, 0)
        th[0, 8 : 8 + IX, :] = th[1, 8 : 8 + IX, :]
        th[NZ + 1, 8 : 8 + IX, :] = th[NZ, 8 : 8 + IX, :]

    def sides(x0, x1, gl, gr):
        a1, b1 = pltpu.roll(x0, 1, 1), pltpu.roll(x1, 1, 1)
        a2, b2 = pltpu.roll(x0, LN - 1, 1), pltpu.roll(x1, LN - 1, 1)
        left = (jnp.where(first, gl, a1), jnp.where(first, a1, b1))
        right = (jnp.where(final, b2, a2), jnp.where(final, gr, b2))
        return left, right

    def int_step(e, src, dst, last):
        def go(m, c):
            for r in range(XC):
                rows = slice(8 * r, 8 * r + 8)
                x = [src[m, 8 + 8 * r : 16 + 8 * r, half] for half in (lo, hi)]
                gl = pltpu.roll(icr[e, 0, rows, :], LN - m, 1)
                gr = pltpu.roll(icr[e, 1, rows, :], LN - 1 - m, 1)
                left, right = sides(x[0], x[1], gl, gr)
                new = []
                for i, half in enumerate((lo, hi)):
                    t = x[i]
                    total = (
                        left[i] + right[i]
                        + src[m, 7 + 8 * r : 15 + 8 * r, half]
                        + src[m, 9 + 8 * r : 17 + 8 * r, half]
                        + src[m - 1, 8 + 8 * r : 16 + 8 * r, half]
                        + src[m + 1, 8 + 8 * r : 16 + 8 * r, half]
                    )
                    alpha = al[m - 1, rows, half]
                    rate = jnp.exp2(C40 * (t * rcp(29.315 + t)))
                    rise = af[m - 1, rows, half] * (0.85 - alpha) * rate
                    out = t + 0.15 * (total - 6.0 * t) + 4.0 * rise
                    al[m - 1, rows, half] = alpha + rise
                    dst[m, 8 + 8 * r : 16 + 8 * r, half] = out
                    new.append(out)
                    if last:
                        put_row(csum.at[r], m, jnp.sum(out, axis=0, keepdims=True), half)
                if not last:
                    int_pack(1, m, r, new[0], new[1])
            return c

        lax.fori_loop(1, NZ + 1, go, 0)

    states = ((hb0, tb0, db0), (hb1, tb1, db1))

    def skin_pack(e, m, r, h, t):
        rows = slice(8 * r, 8 * r + 8)
        for side in range(2):
            sh = m + side
            old = cs[e, side, rows, :]
            new = jnp.where(lane == m, pltpu.roll(h[side], sh, 1), old)
            cs[e, side, rows, :] = jnp.where(lane == m + 64, pltpu.roll(t[side], sh + 64, 1), new)
        for side, at, k in ((0, 0, 0), (1, RC - 1, 7)):
            if r == at:
                for f, x in enumerate((h, t)):
                    for i, half in enumerate((lo, hi)):
                        put_row(rs.at[e, side, f], m, x[i][k : k + 1], half)

    def skin_air(buf):
        H, T, D = buf
        for r in range(RC):
            rows = slice(8 + 8 * r, 16 + 8 * r)
            t = T[DEPTH, rows, :]
            T[DEPTH + 1, rows, :] = t
            D[DEPTH + 1, rows, :] = half_diff(H[DEPTH + 1, rows, :], t)

    def skin_first():
        H, T, D = states[0]
        for r in range(RC):
            rows = slice(8 + 8 * r, 16 + 8 * r)
            for buf in (hb0, hb1):
                buf[0, rows, :] = jnp.ones((8, ARCS), F32)
                buf[DEPTH + 1, rows, :] = amb_ref[8 * r : 8 * r + 8, :]

        def go(m, c):
            for r in range(RC):
                h = [H[m, 8 + 8 * r : 16 + 8 * r, half] for half in (lo, hi)]
                t = [T[m, 8 + 8 * r : 16 + 8 * r, half] for half in (lo, hi)]
                for i, half in enumerate((lo, hi)):
                    d, g = rates(h[i], t[i])
                    D[m, 8 + 8 * r : 16 + 8 * r, half] = d
                    gb[m - 1, 8 * r : 8 * r + 8, half] = g
                skin_pack(0, m, r, h, t)
            return c

        lax.fori_loop(1, DEPTH + 1, go, 0)
        skin_air(states[0])

    def skin_place(k, e, begin, end, wedge):
        H, T, D = states[k % 2]

        @pl.when(ha == 0)
        def _():
            rr[e, 0] = rs[e, 0]

        @pl.when(ha == NH - 1)
        def _():
            rr[e, 1] = rs[e, 1]

        for side in range(2):
            dr[side] = half_diff(rr[e, side, 0], rr[e, side, 1])
            for r in range(RC):
                rows = slice(8 * r, 8 * r + 8)
                x = cr[e, side, rows, :]
                d = half_diff(x, pltpu.roll(x, 64, 1))
                if wedge:
                    new = (lane & 63) <= k
                    x = jnp.where(new, x, ph[k, side, rows, :])
                    d = jnp.where(new, d, pd[k, side, rows, :])
                ph[k, side, rows, :] = x
                pd[k, side, rows, :] = d

        def go(m, c):
            for side, row in ((0, 7), (1, 8 + ROWS)):
                H[m, row : row + 1, :] = rr[e, side, 0, pl.ds(m - 1, 1), :]
                T[m, row : row + 1, :] = rr[e, side, 1, pl.ds(m - 1, 1), :]
                D[m, row : row + 1, :] = dr[side, pl.ds(m - 1, 1), :]
            return c

        lax.fori_loop(begin + 1, end + 1, go, 0)

    def skin_step(k, begin, end, e):
        H, T, D = states[k % 2]
        Hn, Tn, Dn = states[(k + 1) % 2]

        def go(m, c):
            air = jnp.where(m == DEPTH, 2.0, 0.0).astype(F32)
            for r in range(RC):
                rows = slice(8 * r, 8 * r + 8)
                mid = slice(8 + 8 * r, 16 + 8 * r)
                top = slice(7 + 8 * r, 15 + 8 * r)
                bot = slice(9 + 8 * r, 17 + 8 * r)
                h = [H[m, mid, half] for half in (lo, hi)]
                t = [T[m, mid, half] for half in (lo, hi)]
                d = [D[m, mid, half] for half in (lo, hi)]
                pl_, pr_ = ph[k, 0, rows, :], ph[k, 1, rows, :]
                hl, hr = sides(h[0], h[1], pltpu.roll(pl_, LN - m, 1), pltpu.roll(pr_, LN - 1 - m, 1))
                tl, tr = sides(t[0], t[1], pltpu.roll(pl_, 64 - m, 1), pltpu.roll(pr_, 63 - m, 1))
                dl, dr_ = sides(
                    d[0], d[1],
                    pltpu.roll(pd[k, 0, rows, :], LN - m, 1),
                    pltpu.roll(pd[k, 1, rows, :], LN - 1 - m, 1),
                )
                hn, tn = [], []
                for i, half in enumerate((lo, hi)):
                    hc, tc, dc = h[i], t[i], d[i]
                    out = (dc + D[m + 1, mid, half]) * (H[m + 1, mid, half] - hc)
                    moist = (
                        out
                        + (dc + D[m - 1, mid, half]) * (H[m - 1, mid, half] - hc)
                        + (dc + D[m, top, half]) * (H[m, top, half] - hc)
                        + (dc + D[m, bot, half]) * (H[m, bot, half] - hc)
                        + (dc + dl[i]) * (hl[i] - hc)
                        + (dc + dr_[i]) * (hr[i] - hc)
                    )
                    total = (
                        T[m + 1, mid, half] + T[m - 1, mid, half]
                        + T[m, top, half] + T[m, bot, half] + tl[i] + tr[i]
                    )
                    a = ab[m - 1, rows, half]
                    hyd = gb[m - 1, rows, half] * (0.85 - a)
                    h1 = hc + moist - 0.3 * hyd
                    t1 = tc + 0.15 * (total - 6.0 * tc) + 4.0 * hyd + air * out
                    Hn[m, mid, half] = h1
                    Tn[m, mid, half] = t1
                    if k < 3:
                        ab[m - 1, rows, half] = a + hyd
                        d1, g1 = rates(h1, t1)
                        Dn[m, mid, half] = d1
                        gb[m - 1, rows, half] = g1
                    hn.append(h1)
                    tn.append(t1)
                if k < 3:
                    skin_pack(e, m, r, hn, tn)
            return c

        lax.fori_loop(begin + 1, end + 1, go, 0)
        if end == DEPTH and k < 3:
            skin_air(states[(k + 1) % 2])

    def inflow(k):
        T = states[k % 2][1]
        for r in range(RC):
            rows = slice(8 + 8 * r, 16 + 8 * r)
            gain = jnp.sum(T[0, rows, :] - T[1, rows, :], axis=0, keepdims=True)
            if k:
                gain = gain + ub[r : r + 1, :]
            ub[r : r + 1, :] = gain

    to_blk(qs, qr, q_send, q_recv)
    loads[0].wait()

    def pack0(m, c):
        for r in range(XC):
            x = [th0[m, 8 + 8 * r : 16 + 8 * r, half] for half in (lo, hi)]
            int_pack(0, m, r, x[0], x[1])
        return c

    lax.fori_loop(1, NZ + 1, pack0, 0)
    ex_i0 = int_halo(0)
    start(ex_i0)
    loads[1].wait()
    loads[2].wait()
    skin_first()
    ex_s0 = skin_halo(0)
    start(ex_s0)

    loads[3].wait()
    loads[4].wait()
    wait(ex_i0)
    int_place(0, th0)
    int_step(0, th0, th1, False)
    ex_i1 = int_halo(1)
    start(ex_i1)

    loads[5].wait()
    wait(ex_s0)
    skin_place(0, 0, 0, DEPTH, False)
    skin_step(0, 1, DEPTH, BULK[1])
    ex_b1 = skin_halo(BULK[1])
    start(ex_b1)

    wait(ex_i1)
    int_place(1, th1)
    int_step(1, th1, th0, True)
    store_deg = pltpu.make_async_copy(al, deg_out, out_sem.at[0])
    store_deg.start()
    y_i = lax.broadcasted_iota(jnp.int32, (IY, LN), 0)
    c_i = lax.broadcasted_iota(jnp.int32, (IY, LN), 1)

    def mean_matrix(i):
        return jnp.where(((c_i >> 5) == i) & ((c_i & 31) == (y_i >> 3)), 1.0 / 64.0, 0.0).astype(BF16)

    coarse = jnp.zeros((NZ, LN), F32)
    for i in range(XC):
        coarse = coarse + pick(csum[i], mean_matrix(i))
    for i in range(NH):
        csend[i] = coarse[8 * i : 8 * i + 8]
    to_ha(csend, abuf, x1_send, x1_recv)

    from_blk(qs, qr, q_send, q_recv)
    slots = combine(qr)
    for t in range(4):
        key = jnp.broadcast_to(slots[t][0:1], (4 * LN, LN))
        row = lax.broadcasted_iota(jnp.int32, (4 * LN, LN), 0).astype(F32)
        oh[:, t * LN : (t + 1) * LN] = jnp.where(row == key, 1.0, 0.0).astype(BF16)

    wait(ex_b1)
    skin_place(1, BULK[1], 1, DEPTH, False)

    from_ha(csend, abuf, x1_send, x1_recv)
    wide = pick(jnp.concatenate([abuf[i] for i in range(NH)], axis=1), oh[...])
    for t in range(4):
        ws[t] = wide[:, t * LN : (t + 1) * LN]
    to_blk(ws, rbuf, x2_send, x2_recv)

    skin_step(1, 2, DEPTH, BULK[2])
    ex_b2 = skin_halo(BULK[2])
    start(ex_b2)

    from_blk(ws, rbuf, x2_send, x2_recv)
    bound = pick(jnp.concatenate(combine(rbuf), axis=1), o2[...])
    bnd[...] = bound
    bnd_d = half_diff(jnp.ones((8, ARCS), F32), bound)
    for r in range(RC):
        rows = slice(8 + 8 * r, 16 + 8 * r)
        for _, T, D in states:
            T[0, rows, :] = jnp.broadcast_to(bound[r : r + 1], (8, ARCS))
            D[0, rows, :] = jnp.broadcast_to(bnd_d[r : r + 1], (8, ARCS))

    inflow(0)
    skin_step(0, 0, 1, WEDGE[1])
    ex_w1 = skin_halo(WEDGE[1])
    start(ex_w1)
    inflow(1)

    wait(ex_b2)
    skin_place(2, BULK[2], 2, DEPTH, False)
    skin_step(2, 3, DEPTH, BULK[3])
    ex_b3 = skin_halo(BULK[3])
    start(ex_b3)

    wait(ex_w1)
    skin_place(1, WEDGE[1], 0, 1, True)
    skin_step(1, 0, 2, WEDGE[2])
    ex_w2 = skin_halo(WEDGE[2])
    start(ex_w2)
    inflow(2)

    wait(ex_b3)
    skin_place(3, BULK[3], 3, DEPTH, False)
    skin_step(3, 10, DEPTH, None)

    wait(ex_w2)
    skin_place(2, WEDGE[2], 0, 2, True)
    skin_step(2, 0, 3, WEDGE[3])
    ex_w3 = skin_halo(WEDGE[3])
    start(ex_w3)
    inflow(3)
    heat = pick(0.15 * ub[...], o2[...], transpose_b=True)
    for t in range(4):
        vs[t] = heat[:, t * LN : (t + 1) * LN]
    to_blk(vs, vr, u2_send, u2_recv)

    skin_step(3, 4, 10, None)
    wait(ex_w3)
    skin_place(3, WEDGE[3], 0, 3, True)

    from_blk(vs, vr, u2_send, u2_recv)
    summed = pick(jnp.concatenate(combine(vr), axis=1), oh[...], transpose_b=True)
    for i in range(NH):
        ss[i] = summed[:, i * LN : (i + 1) * LN]
    to_ha(ss, ubuf, u1_send, u1_recv)

    skin_step(3, 0, 4, None)
    store_h = pltpu.make_async_copy(hb0.at[slabs, rin, :], hum_out, out_sem.at[1])
    store_t = pltpu.make_async_copy(tb0.at[slabs, rin, :], stemp_out, out_sem.at[2])
    store_h.start()
    store_t.start()

    from_ha(ss, ubuf, u1_send, u1_recv)
    uptake = jnp.concatenate([ubuf[i] for i in range(NH)], axis=0)
    for i in range(XC):
        ge[i] = 0.5 * pick(uptake, mean_matrix(i), transpose_b=True)

    def finish(m, c):
        for r in range(XC):
            mid = slice(8 + 8 * r, 16 + 8 * r)
            th0[m, mid, :] = th0[m, mid, :] - ge[r, pl.ds(m - 1, 1), :]
        return c

    lax.fori_loop(1, NZ + 1, finish, 0)
    store_th = pltpu.make_async_copy(th0.at[layers, xin, :], temp_out, out_sem.at[3])
    store_th.start()
    for copy in (store_deg, store_h, store_t, store_th):
        copy.wait()


def on_device(int_temp, int_degree, int_affinity, hum, stemp, sdeg, ambient, colmap):
    vmem = pltpu.VMEM
    sem = pltpu.SemaphoreType.DMA
    skin_buf = vmem((DEPTH + 2, ROWS + 16, ARCS), F32)
    int_buf = vmem((NZ + 2, IX + 16, IY), F32)
    anywhere = pl.BlockSpec(memory_space=pl.ANY)
    inside = pl.BlockSpec(memory_space=pltpu.VMEM)
    interior = jax.ShapeDtypeStruct((NZ, IX, IY), F32)
    skin = jax.ShapeDtypeStruct((DEPTH, ROWS, ARCS), F32)
    msg = vmem((NB, 8, LN), F32)
    tiles = vmem((4, 8, LN), F32)
    return pl.pallas_call(
        body,
        out_shape=(interior, interior, skin, skin),
        in_specs=[anywhere] * 6 + [inside] * 2,
        out_specs=(anywhere,) * 4,
        scratch_shapes=[
            int_buf, int_buf, vmem((NZ, IX, IY), F32), vmem((NZ, IX, IY), F32),
            skin_buf, skin_buf, skin_buf, skin_buf, skin_buf, skin_buf,
            vmem((DEPTH, ROWS, ARCS), F32), vmem((DEPTH, ROWS, ARCS), F32),
            vmem((N_EX, 2, ROWS, LN), F32), vmem((N_EX, 2, ROWS, LN), F32),
            vmem((N_EX, 2, 2, DEPTH, ARCS), F32), vmem((N_EX, 2, 2, DEPTH, ARCS), F32),
            vmem((4, 2, ROWS, LN), F32), vmem((4, 2, ROWS, LN), F32),
            vmem((2, DEPTH, ARCS), F32),
            vmem((2, 2, IX, LN), F32), vmem((2, 2, IX, LN), F32),
            vmem((2, 2, NZ, IY), F32), vmem((2, 2, NZ, IY), F32),
            tiles, msg, vmem((4 * LN, 4 * LN), BF16), vmem((4 * LN, ARCS), BF16),
            vmem((XC, NZ, IY), F32), tiles, tiles, tiles, msg,
            vmem((8, ARCS), F32), vmem((8, ARCS), F32), tiles, msg, tiles, tiles,
            vmem((XC, NZ, IY), F32),
            sem((6,)), sem((4,)), sem((N_EX + 2, 4)), sem((N_EX + 2, 4)),
            sem((NB,)), sem((NB,)), sem((NH,)), sem((NH,)),
            sem((NB,)), sem((NB,)), sem((NB,)), sem((NB,)), sem((NH,)), sem((NH,)),
        ],
        compiler_params=pltpu.CompilerParams(
            collective_id=0, has_side_effects=True, vmem_limit_bytes=48 * 1024 * 1024
        ),
        name="pylon",
    )(int_temp, int_degree, int_affinity, hum, stemp, sdeg, ambient, colmap.reshape(1, ARCS))


def solution(mesh):
    plan = P(None, "blk", "ha")
    band = P(None, "ha", "blk")
    return jax.shard_map(
        on_device,
        mesh=mesh,
        in_specs=(plan, plan, plan, band, band, band, P("ha", "blk"), P("blk")),
        out_specs=(plan, plan, band, band),
        check_vma=False,
    )
```

time: 1020 us -> 85.3 us (0.08); the launches traced: 1000 us -> 85.1 us
  waiting for transfers between devices: 689 us -> 0 us
  local copies, waits for them, and re-layouts: 127 us -> 6.62 us
  other arithmetic: 104 us -> 0 us
  Pallas kernels: 0 us -> 77.8 us
  starting transfers between devices: 66.7 us -> 0 us
  between operations: 15.6 us -> 0.65 us
    reduce_scatter x1 -> x0, waiting for transfers between devices: 622 us -> none  [on_device(): lax.psum_scatter(flux_rows, ('blk', 'ha'), scatter_dimension=1, tiled=True)]
    pallas_call x0 -> x1, Pallas kernels: none -> 77.8 us  [on_device(): pl.pallas_call(body, out_shape=(interior, interior, skin, skin), in_specs...]
    ppermute x24 -> x0, starting transfers between devices: 66.7 us -> none  [the longest x12 40.6 us: with_halo(): lax.ppermute(lax.slice_in_dim(block, 0, width, axis=dim), axis, backward)]
    scatter x16 -> x0, local copies, waits for them, and re-layouts: 43.3 us -> none  [the longest x2 12.5 us: on_device(): plan_widened.at[:, :, -1]]
    all_gather x1 -> x0, waiting for transfers between devices: 39.4 us -> none  [on_device(): table = lax.all_gather(column_temp, ('blk', 'ha'), axis=1, tiled=True)]
    ppermute x24 -> x0, waiting for transfers between devices: 27.4 us -> none  [the longest x12 21.9 us: with_halo(): lax.ppermute(lax.slice_in_dim(block, 0, width, axis=dim), axis, backward)]
    slice x22 -> x0, local copies, waits for them, and re-layouts: 21.3 us -> none  [the longest x10 9.89 us: with_halo(): lax.slice_in_dim(block, block.shape[dim] - width, None, axis=dim)]
    concatenate x8 -> x0, other arithmetic: 20.6 us -> none  [with_halo(): block = jnp.concatenate([low, block, high], axis=dim)]
  transfers between devices with their start and end apart: 26 -> 0, of which waited for: 15 -> 0; matrix products, arithmetic and copies ran while one was open for 4% -> 0% of each run, Pallas kernels for 0% -> 0%
where the time goes in v1:
time: 85.3 us; the launch traced here: 85.1 us
  Pallas kernels  77.8 us (91%)
  local copies, waits for them, and re-layouts  6.62 us (8%)
    pallas_call x1, Pallas kernels, on_device(): pl.pallas_call(body, out_shape=(interior, interior, skin, skin), in_specs...  77.8 us
    unnamed x10, local copies, waits for them, and re-layouts  6.62 us

profile of v1, /device:TPU:1, one launch (start us, length us, event | category | flops | bytes accessed | tf_op | source)
XLA Modules:
  0.0 85.1 jit_solution(11260539013926383961)
XLA Ops:
  0.6 0.0 copy-start.2
  0.6 0.7 copy-done.2
  1.3 0.0 copy-start
  1.3 1.2 %copy-done = f32[32,32,256]{2,1,0:T(8,128)S(1)} copy-done((f32[32,32,256]{2,1,0:T(8,128)S(1)}, f32[32,32,256]{2,1,0:T(8,128)}, u32[]{:S(2)}) %copy-start) | copy-done | bytes 1048600
  2.5 0.0 copy-start.1
  2.5 0.8 copy-done.1
  3.4 77.8 %pylon.1 = (f32[32,32,256]{2,1,0:T(8,128)S(1)}, f32[32,32,256]{2,1,0:T(8,128)S(1)}, f32[16,64,256]{2,1,0:T(8,128)S(1)}, f32[16,64,256]{2,1,0:T(8,128)S(1)}) custom-call(f32[32,32,256]{2,1,0:T(8,128)S(1)} %copy-done, f32[32,32,256]{2,1,0:T(8,128)} %deg_in.1, f32[32,32,256]{2,1,0:T(8,128)} %aff_in.1, f32[16,64,256]{2,1,0:T(8,128)} %hum_in.1, ...), custom_call_target="tpu_custom_call" | custom-call | tf_op jit(solution)/shard_map/pylon/pallas_call | solution.py:624
  81.2 1.0 %copy.16 = f32[32,32,256]{2,1,0:T(8,128)} copy(f32[32,32,256]{2,1,0:T(8,128)S(1)} %get-tuple-element.8) | data formatting | bytes 2097152
  82.2 1.0 %copy.17 = f32[32,32,256]{2,1,0:T(8,128)} copy(f32[32,32,256]{2,1,0:T(8,128)S(1)} %get-tuple-element.9) | data formatting | bytes 2097152
  83.2 1.0 %copy.18 = f32[16,64,256]{2,1,0:T(8,128)} copy(f32[16,64,256]{2,1,0:T(8,128)S(1)} %get-tuple-element.10) | data formatting | bytes 2097152
  84.1 1.0 %copy.19 = f32[16,64,256]{2,1,0:T(8,128)} copy(f32[16,64,256]{2,1,0:T(8,128)S(1)} %get-tuple-element.11) | data formatting | bytes 2097152
Async XLA Ops:
  0.6 0.7 copy-start.2
  1.3 1.2 %copy-start = (f32[32,32,256]{2,1,0:T(8,128)S(1)}, f32[32,32,256]{2,1,0:T(8,128)}, u32[]{:S(2)}) copy-start(f32[32,32,256]{2,1,0:T(8,128)} %temp_in.1) | copy-start | bytes 3145732
  2.5 0.8 copy-start.1

commit v2 on v1

v2 whole, which is shorter than its diff:
```python
import math

import jax
import jax.numpy as jnp
from jax import lax
from jax.experimental import pallas as pl
from jax.experimental.pallas import tpu as pltpu
from jax.sharding import PartitionSpec as P

F32 = jnp.float32
BF16 = jnp.bfloat16
MESH = pl.DeviceIdType.MESH

NZ, IX, IY = 32, 32, 256
DEPTH, ROWS, ARCS = 16, 64, 256
NB, NH = 32, 4
XC, RC = IX // 8, ROWS // 8
LN = 128

C27 = 2700.0 / 293.15 * math.log2(math.e)
C40 = 4000.0 / 293.15 * math.log2(math.e)

BULK = (0, 1, 2, 3)
WEDGE = (None, 4, 5, 6)
N_EX = 7


def rcp(x):
    r = pl.reciprocal(x, approx=True)
    return r * (2.0 - x * r)


def half_diff(h, t):
    s = 1.0 - h
    s2 = s * s
    s4 = s2 * s2
    q = t * rcp(29.315 + t)
    return (0.00175 + 0.03325 * rcp(1.0 + 65536.0 * (s4 * s4))) * jnp.exp2(C27 * q)


def rates(h, t):
    s = 1.0 - h
    s2 = s * s
    s4 = s2 * s2
    q = t * rcp(29.315 + t)
    d = (0.00175 + 0.03325 * rcp(1.0 + 65536.0 * (s4 * s4))) * jnp.exp2(C27 * q)
    g = 0.08 * rcp(1.0 + 3164.0625 * s4) * jnp.exp2(C40 * q)
    return d, g


def split3(a):
    a1 = a.astype(BF16).astype(F32)
    r1 = a - a1
    a2 = r1.astype(BF16).astype(F32)
    a3 = r1 - a2
    return jnp.concatenate([a1, a2, a3], axis=0).astype(BF16)


def pick(a, b, transpose_b=False):
    rows = a.shape[0]
    dims = (((1,), (1 if transpose_b else 0,)), ((), ()))
    out = lax.dot_general(split3(a), b, dims, preferred_element_type=F32)
    return out[:rows] + out[rows : 2 * rows] + out[2 * rows :]


def both(whole, staged, sems, at, out=False):
    copies = []
    for i in range(2):
        half = slice(i * LN, (i + 1) * LN)
        if len(whole.shape) == 2:
            a, c = whole.at[:, half], staged.at[i]
        else:
            a, c = whole.at[:, :, half], staged.at[:, i]
        src, dst = (c, a) if out else (a, c)
        copies.append(pltpu.make_async_copy(src, dst, sems.at[2 * at + i]))
    return copies


def settle(*refs):
    loads, stores = [], []
    for i in range(4):
        half = refs[i].shape[0] // 2
        for k in range(2):
            part = pl.ds(k * half, half)
            n = 2 * i + k
            via = refs[8 + i].at[part]
            loads.append(pltpu.make_async_copy(refs[i].at[part], via, refs[12].at[n]))
            stores.append(pltpu.make_async_copy(via, refs[4 + i].at[part], refs[13].at[n]))
    for copy in loads:
        copy.start()
    for load, store in zip(loads, stores):
        load.wait()
        store.start()
    for copy in stores:
        copy.wait()


def body(
    temp_in, deg_in, aff_in, hum_in, stemp_in, sdeg_in, amb_in, col_in,
    temp_out, deg_out, hum_out, stemp_out,
    xt, xd, xa, xh, xs, xg, xm, col_ref,
    th0, th1, al, hb0, hb1, tb0, tb1, db0, db1, gb, ab,
    cs, cr, rs, rr, cg, dr, ics, icr, icg, irs, irr,
    qs, qr, oh, o2, csum, csend, abuf, ws, rbuf, ub, vs, vr, ss, ubuf, ge,
    in_sem, out_sem, hs_send, hs_recv, q_send, q_recv, x1_send, x1_recv,
    x2_send, x2_recv, u2_send, u2_recv, u1_send, u1_recv,
):
    b = lax.axis_index("blk")
    ha = lax.axis_index("ha")
    lane = lax.broadcasted_iota(jnp.int32, (8, LN), 1)
    first = lane == 0
    final = lane == LN - 1
    lo, hi = slice(0, LN), slice(LN, 2 * LN)

    halves = (lo, hi)

    col_load = pltpu.make_async_copy(col_in, col_ref, in_sem.at[14])
    col_load.start()
    loads = [
        both(src, dst, in_sem, i)
        for i, (src, dst) in enumerate(
            [
                (temp_in, xt), (hum_in, xh), (stemp_in, xs), (amb_in, xm),
                (aff_in, xa), (deg_in, xd), (sdeg_in, xg),
            ]
        )
    ]
    for copies in loads:
        for copy in copies:
            copy.start()

    barrier = pltpu.get_barrier_semaphore()

    def greet(k, c):
        pl.semaphore_signal(barrier, inc=1, device_id=(lax.rem(b + k, NB), ha), device_id_type=MESH)
        return c

    lax.fori_loop(1, NB, greet, 0)
    for k in range(1, NH):
        pl.semaphore_signal(barrier, inc=1, device_id=(b, lax.rem(ha + k, NH)), device_id_type=MESH)

    col_load.wait()

    col = col_ref[...]
    owner = col >> 7
    colf = jnp.broadcast_to(owner.astype(F32), (ARCS, ARCS))
    owner_down = colf.T
    q_i = lax.broadcasted_iota(jnp.int32, (ARCS, ARCS), 0)
    p_i = lax.broadcasted_iota(jnp.int32, (ARCS, ARCS), 1)
    earlier = jnp.where((owner_down == colf) & (q_i < p_i), 1.0, 0.0)
    rank = jnp.sum(earlier, axis=0, keepdims=True).astype(jnp.int32)
    ob = col >> 9
    pos = (ob >> 3) * LN + (((ob + b) & 7) << 4) + ((owner & 3) << 2) + rank
    posf = pos.astype(F32)
    pos_down = jnp.broadcast_to(posf, (LN, ARCS)).T
    val_down = jnp.broadcast_to((col & 511).astype(F32) + 1.0, (LN, ARCS)).T
    lanes_a = lax.broadcasted_iota(jnp.int32, (ARCS, LN), 1).astype(F32)
    for t in range(4):
        hit = jnp.where(pos_down == lanes_a + float(t * LN), val_down, 0.0)
        qs[t] = jnp.broadcast_to(jnp.sum(hit, axis=0, keepdims=True) - 1.0, (8, LN))
    slot_i = lax.broadcasted_iota(jnp.int32, (4 * LN, ARCS), 0).astype(F32)
    o2[...] = jnp.where(slot_i == posf, 1.0, 0.0).astype(BF16)

    zero = jnp.zeros((8, LN), F32)

    def clear(e, c):
        for side in range(2):
            for r in range(RC):
                cs[e, r] = zero
            for f in range(2):
                rs[e, side, f] = jnp.zeros((DEPTH, ARCS), F32)
        return c

    lax.fori_loop(0, N_EX, clear, 0)
    for e in range(2):
        for r in range(XC):
            ics[e, r] = zero

    pl.semaphore_wait(barrier, NB - 1 + NH - 1)

    def to_blk(src, dst, send, recv):
        def go(k, c):
            to = lax.rem(b + k, NB)
            pltpu.make_async_remote_copy(
                src_ref=src.at[to // 8], dst_ref=dst.at[b], send_sem=send.at[to],
                recv_sem=recv.at[b], device_id=(to, ha), device_id_type=MESH,
            ).start()
            return c

        lax.fori_loop(1, NB, go, 0)

    def from_blk(src, dst, send, recv):
        def go(k, c):
            other = lax.rem(b + k, NB)
            copy = pltpu.make_async_remote_copy(
                src_ref=src.at[other // 8], dst_ref=dst.at[other], send_sem=send.at[other],
                recv_sem=recv.at[other], device_id=(other, ha), device_id_type=MESH,
            )
            copy.wait_send()
            copy.wait_recv()
            return c

        lax.fori_loop(1, NB, go, 0)
        dst[b] = src[b // 8]

    def combine(buf):
        tiles = []
        for t in range(4):
            acc = zero
            for j in range(8):
                acc = jnp.where((lane >> 4) == ((b + j) & 7), buf[t * 8 + j], acc)
            tiles.append(acc)
        return tiles

    def to_ha(src, dst, send, recv):
        for k in range(1, NH):
            to = lax.rem(ha + k, NH)
            pltpu.make_async_remote_copy(
                src_ref=src.at[to], dst_ref=dst.at[ha], send_sem=send.at[to],
                recv_sem=recv.at[ha], device_id=(b, to), device_id_type=MESH,
            ).start()

    def from_ha(src, dst, send, recv):
        for k in range(1, NH):
            other = lax.rem(ha + k, NH)
            copy = pltpu.make_async_remote_copy(
                src_ref=src.at[other], dst_ref=dst.at[other], send_sem=send.at[other],
                recv_sem=recv.at[other], device_id=(b, other), device_id_type=MESH,
            )
            copy.wait_send()
            copy.wait_recv()
        dst[ha] = src[ha]

    b_dn, b_up = lax.rem(b + NB - 1, NB), lax.rem(b + 1, NB)
    h_dn, h_up = lax.rem(ha + NH - 1, NH), lax.rem(ha + 1, NH)

    def halo(e, src_blk, dst_blk, src_ha, dst_ha):
        return [
            pltpu.make_async_remote_copy(
                src_ref=src, dst_ref=dst, send_sem=hs_send.at[e, i],
                recv_sem=hs_recv.at[e, i], device_id=dev, device_id_type=MESH,
            )
            for i, (src, dst, dev) in enumerate(
                [
                    (src_blk[0], dst_blk.at[1], (b_dn, ha)),
                    (src_blk[1], dst_blk.at[0], (b_up, ha)),
                    (src_ha[0], dst_ha.at[1], (b, h_dn)),
                    (src_ha[1], dst_ha.at[0], (b, h_up)),
                ]
            )
        ]

    def skin_halo(e):
        cols, rows = cs.at[e], rs.at[e]
        return halo(e, (cols, cols), cr.at[e], (rows.at[0], rows.at[1]), rr.at[e])

    def int_halo(e):
        cols, rows = ics.at[e], irs.at[e]
        return halo(N_EX + e, (rows.at[0], rows.at[1]), irr.at[e], (cols, cols), icr.at[e])

    def sweep(go, begin, end):
        count = end - begin

        def two(i, c):
            go(begin + 2 * i)
            go(begin + 2 * i + 1)
            return c

        if count > 1:
            lax.fori_loop(0, count // 2, two, 0)
        if count % 2:
            go(end - 1)

    def start(copies):
        for copy in copies:
            copy.start()

    def wait(copies):
        for copy in copies:
            copy.wait()

    sub = lax.broadcasted_iota(jnp.int32, (8, LN), 0)

    def put_row(ref, m, row, half):
        tile = pl.ds(pl.multiple_of(((m - 1) // 8) * 8, 8), 8)
        here = sub == lax.rem(m - 1, 8)
        ref[tile, half] = jnp.where(here, jnp.broadcast_to(row, (8, LN)), ref[tile, half])

    pair = (lane + 1) >> 1
    odd = (lane & 1) == 1
    def shift_rows(x, ghost_row, up):
        ghost = jnp.broadcast_to(ghost_row, (8, LN))
        if up:
            return jnp.where(sub == 0, ghost, pltpu.roll(x, 1, 0))
        return jnp.where(sub == 7, ghost, pltpu.roll(x, 7, 0))

    def int_pack(e, m, r, x, mine):
        edge = pltpu.roll(jnp.where(final, x[1], x[0]), 2 * m, 1)
        ics[e, r] = jnp.where(mine, edge, ics[e, r])
        for side, at, k in ((0, 0, 0), (1, XC - 1, 7)):
            if r == at:
                for i, half in enumerate(halves):
                    put_row(irs.at[e, side], m, x[i][k : k + 1], half)

    def int_place(e, th):
        @pl.when(b == 0)
        def _():
            irr[e, 0] = irs[e, 0]

        @pl.when(b == NB - 1)
        def _():
            irr[e, 1] = irs[e, 1]

        at_low = jnp.full((8, LN), ha, jnp.int32) == 0
        at_high = jnp.full((8, LN), ha, jnp.int32) == NH - 1
        for r in range(XC):
            own = pltpu.roll(ics[e, r], LN - 1, 1)
            low = jnp.where(at_low, own, icr[e, 0, r])
            high = jnp.where(at_high, own, pltpu.roll(icr[e, 1, r], LN - 2, 1))
            icg[e, r] = jnp.where(odd, low, high)
            th[0, r] = th[1, r]
            th[NZ + 1, r] = th[NZ, r]

    def sides(x0, x1, ghost):
        a1, b1 = pltpu.roll(x0, 1, 1), pltpu.roll(x1, 1, 1)
        a2, b2 = pltpu.roll(x0, LN - 1, 1), pltpu.roll(x1, LN - 1, 1)
        left = (jnp.where(first, ghost, a1), jnp.where(first, a1, b1))
        right = (jnp.where(final, b2, a2), jnp.where(final, ghost, b2))
        return left, right

    def int_step(e, src, dst, last):
        def go(m):
            mine = pair == m
            sums = [0.0, 0.0]
            for r in range(XC):
                part = pl.ds(r, 8, stride=XC)
                x = [src[m, r, :, half] for half in halves]
                left, right = sides(x[0], x[1], pltpu.roll(icg[e, r], 129 - 2 * m, 1))
                new = []
                for i, half in enumerate(halves):
                    t = x[i]
                    if r == 0:
                        up = shift_rows(src[m, XC - 1, :, half], irr[e, 0, pl.ds(m - 1, 1), :][:, half], True)
                    else:
                        up = src[m, r - 1, :, half]
                    if r == XC - 1:
                        down = shift_rows(src[m, 0, :, half], irr[e, 1, pl.ds(m - 1, 1), :][:, half], False)
                    else:
                        down = src[m, r + 1, :, half]
                    total = (left[i] + right[i]) + (up + down) + (
                        src[m - 1, r, :, half] + src[m + 1, r, :, half]
                    )
                    alpha = al[m - 1, r, :, half] if last else xd[m - 1, i, part, :]
                    rate = jnp.exp2(C40 * (t * rcp(29.315 + t)))
                    rise = xa[m - 1, i, part, :] * (0.85 - alpha) * rate
                    out = t + 0.15 * (total - 6.0 * t) + 4.0 * rise
                    if last:
                        xd[m - 1, i, part, :] = alpha + rise
                        sums[i] = sums[i] + out
                    else:
                        al[m - 1, r, :, half] = alpha + rise
                    dst[m, r, :, half] = out
                    new.append(out)
                if not last:
                    int_pack(1, m, r, new, mine)
            if last:
                for i, half in enumerate(halves):
                    both = sums[i] + pltpu.roll(sums[i], 7, 0)
                    for r in range(XC):
                        put_row(csum.at[r], m, both[2 * r : 2 * r + 1], half)

        sweep(go, 1, NZ + 1)

    states = ((hb0, tb0, db0), (hb1, tb1, db1))

    def skin_pack(e, m, r, h, t, mine_h, mine_t):
        eh = pltpu.roll(jnp.where(final, h[1], h[0]), 2 * m, 1)
        et = pltpu.roll(jnp.where(final, t[1], t[0]), 2 * m + 40, 1)
        cs[e, r] = jnp.where(mine_t, et, jnp.where(mine_h, eh, cs[e, r]))
        for side, at, k in ((0, 0, 0), (1, RC - 1, 7)):
            if r == at:
                for f, x in enumerate((h, t)):
                    for i, half in enumerate(halves):
                        put_row(rs.at[e, side, f], m, x[i][k : k + 1], half)

    def skin_air(buf):
        H, T, D = buf
        for r in range(RC):
            t = T[DEPTH, r]
            T[DEPTH + 1, r] = t
            D[DEPTH + 1, r] = half_diff(H[DEPTH + 1, r], t)

    def skin_first():
        H, T, D = states[0]
        for r in range(RC):
            for i, half in enumerate(halves):
                air = xm[i, pl.ds(r, 8, stride=RC), :]
                for buf in (hb0, hb1):
                    buf[0, r, :, half] = jnp.ones((8, LN), F32)
                    buf[DEPTH + 1, r, :, half] = air

        def go(m, c):
            mine_h, mine_t = pair == m, pair == m + 20
            for r in range(RC):
                part = pl.ds(r, 8, stride=RC)
                h = [xh[m - 1, i, part, :] for i in range(2)]
                t = [xs[m - 1, i, part, :] for i in range(2)]
                for i, half in enumerate(halves):
                    d, g = rates(h[i], t[i])
                    H[m, r, :, half] = h[i]
                    T[m, r, :, half] = t[i]
                    D[m, r, :, half] = d
                    gb[m - 1, r, :, half] = g
                skin_pack(0, m, r, h, t, mine_h, mine_t)
            return c

        lax.fori_loop(1, DEPTH + 1, go, 0)
        skin_air(states[0])

    def skin_place(k, e, wedge):
        @pl.when(ha == 0)
        def _():
            rr[e, 0] = rs[e, 0]

        @pl.when(ha == NH - 1)
        def _():
            rr[e, 1] = rs[e, 1]

        if wedge:
            here = lax.broadcasted_iota(jnp.int32, (DEPTH, ARCS), 0) >= k
            for side in range(2):
                for f in range(2):
                    rr[e, side, f] = jnp.where(here, rr[BULK[k], side, f], rr[e, side, f])
        for side in range(2):
            dr[e, side] = half_diff(rr[e, side, 0], rr[e, side, 1])
        field = jnp.where(lane >= 80, lane - 80, jnp.where(lane >= 40, lane - 40, lane))
        fresh = (field >> 1) < k
        for r in range(RC):
            x = jnp.where(odd, cr[e, 0, r], pltpu.roll(cr[e, 1, r], LN - 2, 1))
            d = half_diff(x, pltpu.roll(x, LN - 40, 1))
            x = jnp.where(lane >= 80, pltpu.roll(d, 80, 1), x)
            cg[k, r] = jnp.where(fresh, x, cg[k, r]) if wedge else x

    def skin_step(k, begin, end, e, e_in):
        H, T, D = states[k % 2]
        Hn, Tn, Dn = states[(k + 1) % 2]

        def go(m):
            mine_h, mine_t = pair == m, pair == m + 20
            air = jnp.where(m == DEPTH, 2.0, 0.0)
            row = pl.ds(m - 1, 1)
            flow = [0.0, 0.0]
            for r in range(RC):
                part = pl.ds(r, 8, stride=RC)
                ghosts = cg[k, r]
                h = [H[m, r, :, half] for half in halves]
                t = [T[m, r, :, half] for half in halves]
                d = [D[m, r, :, half] for half in halves]
                gh, gt, gd = (pltpu.roll(ghosts, at - 2 * m, 1) for at in (129, 89, 49))
                tl, tr = sides(t[0], t[1], gt)
                h0, h1 = pltpu.roll(h[0], LN - 1, 1), pltpu.roll(h[1], LN - 1, 1)
                d0, d1 = pltpu.roll(d[0], LN - 1, 1), pltpu.roll(d[1], LN - 1, 1)
                f0 = (d[0] + jnp.where(final, d1, d0)) * (jnp.where(final, h1, h0) - h[0])
                f1 = (d[1] + jnp.where(final, gd, d1)) * (jnp.where(final, gh, h1) - h[1])
                s0, s1 = pltpu.roll(f0, 1, 1), pltpu.roll(f1, 1, 1)
                across = (
                    f0 - jnp.where(first, (d[0] + gd) * (h[0] - gh), s0),
                    f1 - jnp.where(first, s0, s1),
                )
                hn, tn = [], []
                for i, half in enumerate(halves):
                    hc, tc, dc = h[i], t[i], d[i]
                    if r == 0:
                        hu, tu, du = (
                            shift_rows(x[m, RC - 1, :, half], g[row, :][:, half], True)
                            for x, g in ((H, rr.at[e_in, 0, 0]), (T, rr.at[e_in, 0, 1]), (D, dr.at[e_in, 0]))
                        )
                        flow[i] = (du + dc) * (hc - hu)
                    else:
                        tu = T[m, r - 1, :, half]
                    if r == RC - 1:
                        hd, td, dd = (
                            shift_rows(x[m, 0, :, half], g[row, :][:, half], False)
                            for x, g in ((H, rr.at[e_in, 1, 0]), (T, rr.at[e_in, 1, 1]), (D, dr.at[e_in, 1]))
                        )
                    else:
                        hd, td, dd = H[m, r + 1, :, half], T[m, r + 1, :, half], D[m, r + 1, :, half]
                    below = (dc + dd) * (hd - hc)
                    out = (dc + D[m + 1, r, :, half]) * (H[m + 1, r, :, half] - hc)
                    into = (dc + D[m - 1, r, :, half]) * (H[m - 1, r, :, half] - hc)
                    moist = (out + into) + (below - flow[i]) + across[i]
                    flow[i] = below
                    total = (T[m + 1, r, :, half] + T[m - 1, r, :, half]) + (tu + td) + (tl[i] + tr[i])
                    a = xg[m - 1, i, part, :] if k == 0 else ab[m - 1, r, :, half]
                    hyd = gb[m - 1, r, :, half] * (0.85 - a)
                    h1_ = hc + moist - 0.3 * hyd
                    t1_ = tc + 0.15 * (total - 6.0 * tc) + 4.0 * hyd + air * out
                    if k < 3:
                        Hn[m, r, :, half] = h1_
                        Tn[m, r, :, half] = t1_
                        ab[m - 1, r, :, half] = a + hyd
                        dn, gn = rates(h1_, t1_)
                        Dn[m, r, :, half] = dn
                        gb[m - 1, r, :, half] = gn
                    else:
                        xh[m - 1, i, part, :] = h1_
                        xs[m - 1, i, part, :] = t1_
                    hn.append(h1_)
                    tn.append(t1_)
                if k < 3:
                    skin_pack(e, m, r, hn, tn, mine_h, mine_t)

        sweep(go, begin + 1, end + 1)
        if end == DEPTH and k < 3:
            skin_air(states[(k + 1) % 2])

    def inflow(k):
        T = states[k % 2][1]
        gain = 0.0 if k == 0 else ub[...]
        for r in range(RC):
            gain = gain + (T[0, r] - T[1, r])
        ub[...] = gain

    wait(loads[0])

    def pack0(m, c):
        mine = pair == m
        for r in range(XC):
            x = [xt[m - 1, i, pl.ds(r, 8, stride=XC), :] for i in range(2)]
            for i, half in enumerate(halves):
                th0[m, r, :, half] = x[i]
            int_pack(0, m, r, x, mine)
        return c

    lax.fori_loop(1, NZ + 1, pack0, 0, unroll=2)
    ex_i0 = int_halo(0)
    start(ex_i0)
    to_blk(qs, qr, q_send, q_recv)
    for i in (1, 2, 3):
        wait(loads[i])
    skin_first()
    ex_s0 = skin_halo(0)
    start(ex_s0)

    wait(loads[4])
    wait(loads[5])
    wait(ex_i0)
    int_place(0, th0)
    int_step(0, th0, th1, False)
    ex_i1 = int_halo(1)
    start(ex_i1)

    wait(loads[6])
    wait(ex_s0)
    skin_place(0, 0, False)
    skin_step(0, 1, DEPTH, BULK[1], BULK[0])
    ex_b1 = skin_halo(BULK[1])
    start(ex_b1)

    wait(ex_i1)
    int_place(1, th1)
    int_step(1, th1, th0, True)
    store_deg = both(deg_out, xd, out_sem, 0, True)
    start(store_deg)
    y_i = lax.broadcasted_iota(jnp.int32, (IY, LN), 0)
    c_i = lax.broadcasted_iota(jnp.int32, (IY, LN), 1)

    def mean_matrix(i):
        return jnp.where(((c_i >> 5) == i) & ((c_i & 31) == (y_i >> 3)), 1.0 / 64.0, 0.0).astype(BF16)

    coarse = jnp.zeros((NZ, LN), F32)
    for i in range(XC):
        coarse = coarse + pick(csum[i], mean_matrix(i))
    for i in range(NH):
        csend[i] = coarse[8 * i : 8 * i + 8]
    to_ha(csend, abuf, x1_send, x1_recv)

    from_blk(qs, qr, q_send, q_recv)
    slots = combine(qr)
    for t in range(4):
        key = jnp.broadcast_to(slots[t][0:1], (4 * LN, LN))
        row = lax.broadcasted_iota(jnp.int32, (4 * LN, LN), 0).astype(F32)
        oh[:, t * LN : (t + 1) * LN] = jnp.where(row == key, 1.0, 0.0).astype(BF16)

    wait(ex_b1)
    skin_place(1, BULK[1], False)

    from_ha(csend, abuf, x1_send, x1_recv)
    wide = pick(jnp.concatenate([abuf[i] for i in range(NH)], axis=1), oh[...])
    for t in range(4):
        ws[t] = wide[:, t * LN : (t + 1) * LN]
    to_blk(ws, rbuf, x2_send, x2_recv)

    skin_step(1, 2, DEPTH, BULK[2], BULK[1])
    ex_b2 = skin_halo(BULK[2])
    start(ex_b2)

    from_blk(ws, rbuf, x2_send, x2_recv)
    bound = pick(jnp.concatenate(combine(rbuf), axis=1), o2[...])
    bound_d = half_diff(jnp.ones((8, ARCS), F32), bound)
    for r in range(RC):
        for _, T, D in states:
            T[0, r] = bound
            D[0, r] = bound_d

    inflow(0)
    skin_step(0, 0, 1, WEDGE[1], BULK[0])
    ex_w1 = skin_halo(WEDGE[1])
    start(ex_w1)
    inflow(1)

    wait(ex_b2)
    skin_place(2, BULK[2], False)
    skin_step(2, 3, DEPTH, BULK[3], BULK[2])
    ex_b3 = skin_halo(BULK[3])
    start(ex_b3)

    wait(ex_w1)
    skin_place(1, WEDGE[1], True)
    skin_step(1, 0, 2, WEDGE[2], WEDGE[1])
    ex_w2 = skin_halo(WEDGE[2])
    start(ex_w2)
    inflow(2)

    wait(ex_b3)
    skin_place(3, BULK[3], False)
    skin_step(3, 10, DEPTH, None, BULK[3])

    wait(ex_w2)
    skin_place(2, WEDGE[2], True)
    skin_step(2, 0, 3, WEDGE[3], WEDGE[2])
    ex_w3 = skin_halo(WEDGE[3])
    start(ex_w3)
    inflow(3)
    heat = pick(0.15 * ub[...], o2[...], transpose_b=True)
    for t in range(4):
        vs[t] = heat[:, t * LN : (t + 1) * LN]
    to_blk(vs, vr, u2_send, u2_recv)

    skin_step(3, 4, 10, None, BULK[3])
    wait(ex_w3)
    skin_place(3, WEDGE[3], True)

    from_blk(vs, vr, u2_send, u2_recv)
    summed = pick(jnp.concatenate(combine(vr), axis=1), oh[...], transpose_b=True)
    for i in range(NH):
        ss[i] = summed[:, i * LN : (i + 1) * LN]
    to_ha(ss, ubuf, u1_send, u1_recv)

    skin_step(3, 0, 4, None, WEDGE[3])
    store_h = both(hum_out, xh, out_sem, 1, True)
    store_t = both(stemp_out, xs, out_sem, 2, True)
    start(store_h)
    start(store_t)

    from_ha(ss, ubuf, u1_send, u1_recv)
    uptake = jnp.concatenate([ubuf[i] for i in range(NH)], axis=0)
    for i in range(XC):
        ge[i] = 0.5 * pick(uptake, mean_matrix(i), transpose_b=True)

    def finish(m, c):
        for i, half in enumerate(halves):
            cool = jnp.zeros((8, LN), F32)
            for g in range(XC):
                row = jnp.broadcast_to(ge[g, pl.ds(m - 1, 1), :][:, half], (8, LN))
                cool = jnp.where((sub >> 1) == g, row, cool)
            for r in range(XC):
                xt[m - 1, i, pl.ds(r, 8, stride=XC), :] = th0[m, r, :, half] - cool
        return c

    lax.fori_loop(1, NZ + 1, finish, 0, unroll=2)
    store_th = both(temp_out, xt, out_sem, 3, True)
    start(store_th)
    for copies in (store_deg, store_h, store_t, store_th):
        wait(copies)


def on_device(int_temp, int_degree, int_affinity, hum, stemp, sdeg, ambient, colmap):
    vmem = pltpu.VMEM
    sem = pltpu.SemaphoreType.DMA
    skin_buf = vmem((DEPTH + 2, RC, 8, ARCS), F32)
    int_buf = vmem((NZ + 2, XC, 8, IY), F32)
    int_stage = vmem((NZ, 2, IX, LN), F32)
    skin_stage = vmem((DEPTH, 2, ROWS, LN), F32)
    outside = pl.BlockSpec(memory_space=pltpu.HBM)
    interior = jax.ShapeDtypeStruct((NZ, IX, IY), F32)
    skin = jax.ShapeDtypeStruct((DEPTH, ROWS, ARCS), F32)
    outs = (interior, interior, skin, skin)
    msg = vmem((NB, 8, LN), F32)
    tiles = vmem((4, 8, LN), F32)
    results = pl.pallas_call(
        body,
        out_shape=outs,
        in_specs=[outside] * 8,
        out_specs=(outside,) * 4,
        scratch_shapes=[
            int_stage, int_stage, int_stage, skin_stage, skin_stage, skin_stage,
            vmem((2, ROWS, LN), F32), vmem((1, ARCS), jnp.int32),
            int_buf, int_buf, vmem((NZ, XC, 8, IY), F32),
            skin_buf, skin_buf, skin_buf, skin_buf, skin_buf, skin_buf,
            vmem((DEPTH, RC, 8, ARCS), F32), vmem((DEPTH, RC, 8, ARCS), F32),
            vmem((N_EX, RC, 8, LN), F32), vmem((N_EX, 2, RC, 8, LN), F32),
            vmem((N_EX, 2, 2, DEPTH, ARCS), F32), vmem((N_EX, 2, 2, DEPTH, ARCS), F32),
            vmem((4, RC, 8, LN), F32), vmem((N_EX, 2, DEPTH, ARCS), F32),
            vmem((2, XC, 8, LN), F32), vmem((2, 2, XC, 8, LN), F32), vmem((2, XC, 8, LN), F32),
            vmem((2, 2, NZ, IY), F32), vmem((2, 2, NZ, IY), F32),
            tiles, msg, vmem((4 * LN, 4 * LN), BF16), vmem((4 * LN, ARCS), BF16),
            vmem((XC, NZ, IY), F32), tiles, tiles, tiles, msg,
            vmem((8, ARCS), F32), tiles, msg, tiles, tiles,
            vmem((XC, NZ, IY), F32),
            sem((15,)), sem((8,)), sem((N_EX + 2, 4)), sem((N_EX + 2, 4)),
            sem((NB,)), sem((NB,)), sem((NH,)), sem((NH,)),
            sem((NB,)), sem((NB,)), sem((NB,)), sem((NB,)), sem((NH,)), sem((NH,)),
        ],
        compiler_params=pltpu.CompilerParams(
            collective_id=0, has_side_effects=True, vmem_limit_bytes=59 * 1024 * 1024
        ),
        name="pylon",
    )(int_temp, int_degree, int_affinity, hum, stemp, sdeg, ambient, colmap.reshape(1, ARCS))
    return pl.pallas_call(
        settle,
        out_shape=outs,
        in_specs=[outside] * 4,
        out_specs=(outside,) * 4,
        scratch_shapes=[vmem(x.shape, F32) for x in outs] + [sem((8,)), sem((8,))],
        compiler_params=pltpu.CompilerParams(vmem_limit_bytes=59 * 1024 * 1024),
        name="settle",
    )(*results)


def solution(mesh):
    plan = P(None, "blk", "ha")
    band = P(None, "ha", "blk")
    return jax.shard_map(
        on_device,
        mesh=mesh,
        in_specs=(plan, plan, plan, band, band, band, P("ha", "blk"), P("blk")),
        out_specs=(plan, plan, band, band),
        check_vma=False,
    )
```

time: 85.3 us -> 76 us (0.89)
  local copies, waits for them, and re-layouts: 6.62 us -> 0 us
  Pallas kernels: 77.8 us -> 75.2 us
    unnamed x10 -> x0, local copies, waits for them, and re-layouts: 6.62 us -> none
    pallas_call x1 -> x2, Pallas kernels: 77.8 us -> 75.2 us  [the longest x1 71.6 us: on_device(): pl.pallas_call(body, out_shape=outs, in_specs=[outside] * 8, out_specs=(o...]
where the time goes in v2:
time: 76 us; the launch traced here: 75.8 us
  Pallas kernels  75.2 us (99%)
    pallas_call x1, Pallas kernels, on_device(): pl.pallas_call(body, out_shape=outs, in_specs=[outside] * 8, out_specs=(o...  71.6 us
    pallas_call x1, Pallas kernels, on_device(): pl.pallas_call(settle, out_shape=outs, in_specs=[outside] * 4, out_specs=...  3.58 us

profile of v2, /device:TPU:1, one launch (start us, length us, event | category | flops | bytes accessed | tf_op | source)
XLA Modules:
  0.0 75.8 jit_solution(2198200925741078161)
XLA Ops:
  0.6 71.6 %pylon.1 = (f32[32,32,256]{2,1,0:T(8,128)}, f32[32,32,256]{2,1,0:T(8,128)}, f32[16,64,256]{2,1,0:T(8,128)}, f32[16,64,256]{2,1,0:T(8,128)}) custom-call(f32[32,32,256]{2,1,0:T(8,128)} %temp_in.1, f32[32,32,256]{2,1,0:T(8,128)} %deg_in.1, f32[32,32,256]{2,1,0:T(8,128)} %aff_in.1, f32[16,64,256]{2,1,0:T(8,128)} %hum_in.1, f32[16,64,256]{2,1,0:T(8,128)} %stemp_in.1, ...), custom_call_target="tpu_custom_call" | custom-call | tf_op jit(solution)/shard_map/pylon/pallas_call | solution.py:691
  72.3 3.6 %settle.1 = (f32[32,32,256]{2,1,0:T(8,128)}, f32[32,32,256]{2,1,0:T(8,128)}, f32[16,64,256]{2,1,0:T(8,128)}, f32[16,64,256]{2,1,0:T(8,128)}) custom-call(f32[32,32,256]{2,1,0:T(8,128)} %get-tuple-element.8.refs_0_, f32[32,32,256]{2,1,0:T(8,128)} %get-tuple-element.9.refs_1_, f32[16,64,256]{2,1,0:T(8,128)} %get-tuple-element.10.refs_2_, ...), custom_call_target="tpu_custom_call" | custom-call | tf_op jit(solution)/shard_map/settle/pallas_call | solution.py:720

commit v3 on v2

--- a/solution.py
+++ b/solution.py
@@ -77,32 +77,23 @@
 
 
 def settle(*refs):
-    loads, stores = [], []
+    copies = []
     for i in range(4):
-        half = refs[i].shape[0] // 2
-        for k in range(2):
-            part = pl.ds(k * half, half)
-            n = 2 * i + k
-            via = refs[8 + i].at[part]
-            loads.append(pltpu.make_async_copy(refs[i].at[part], via, refs[12].at[n]))
-            stores.append(pltpu.make_async_copy(via, refs[4 + i].at[part], refs[13].at[n]))
-    for copy in loads:
+        copies += both(refs[4 + i], refs[i], refs[8], i, True)
+    for copy in copies:
         copy.start()
-    for load, store in zip(loads, stores):
-        load.wait()
-        store.start()
-    for copy in stores:
+    for copy in copies:
         copy.wait()
 
 
 def body(
     temp_in, deg_in, aff_in, hum_in, stemp_in, sdeg_in, amb_in, col_in,
-    temp_out, deg_out, hum_out, stemp_out,
-    xt, xd, xa, xh, xs, xg, xm, col_ref,
+    xt, xd, xh, xs,
+    xa, xg, xm, col_ref,
     th0, th1, al, hb0, hb1, tb0, tb1, db0, db1, gb, ab,
     cs, cr, rs, rr, cg, dr, ics, icr, icg, irs, irr,
     qs, qr, oh, o2, csum, csend, abuf, ws, rbuf, ub, vs, vr, ss, ubuf, ge,
-    in_sem, out_sem, hs_send, hs_recv, q_send, q_recv, x1_send, x1_recv,
+    in_sem, hs_send, hs_recv, q_send, q_recv, x1_send, x1_recv,
     x2_send, x2_recv, u2_send, u2_recv, u1_send, u1_recv,
 ):
     b = lax.axis_index("blk")
@@ -111,6 +102,7 @@
     first = lane == 0
     final = lane == LN - 1
     lo, hi = slice(0, LN), slice(LN, 2 * LN)
+    zero = jnp.zeros((8, LN), F32)
 
     halves = (lo, hi)
 
@@ -139,48 +131,9 @@
     for k in range(1, NH):
         pl.semaphore_signal(barrier, inc=1, device_id=(b, lax.rem(ha + k, NH)), device_id_type=MESH)
 
-    col_load.wait()
-
-    col = col_ref[...]
-    owner = col >> 7
-    colf = jnp.broadcast_to(owner.astype(F32), (ARCS, ARCS))
-    owner_down = colf.T
-    q_i = lax.broadcasted_iota(jnp.int32, (ARCS, ARCS), 0)
-    p_i = lax.broadcasted_iota(jnp.int32, (ARCS, ARCS), 1)
-    earlier = jnp.where((owner_down == colf) & (q_i < p_i), 1.0, 0.0)
-    rank = jnp.sum(earlier, axis=0, keepdims=True).astype(jnp.int32)
-    ob = col >> 9
-    pos = (ob >> 3) * LN + (((ob + b) & 7) << 4) + ((owner & 3) << 2) + rank
-    posf = pos.astype(F32)
-    pos_down = jnp.broadcast_to(posf, (LN, ARCS)).T
-    val_down = jnp.broadcast_to((col & 511).astype(F32) + 1.0, (LN, ARCS)).T
-    lanes_a = lax.broadcasted_iota(jnp.int32, (ARCS, LN), 1).astype(F32)
-    for t in range(4):
-        hit = jnp.where(pos_down == lanes_a + float(t * LN), val_down, 0.0)
-        qs[t] = jnp.broadcast_to(jnp.sum(hit, axis=0, keepdims=True) - 1.0, (8, LN))
-    slot_i = lax.broadcasted_iota(jnp.int32, (4 * LN, ARCS), 0).astype(F32)
-    o2[...] = jnp.where(slot_i == posf, 1.0, 0.0).astype(BF16)
-
-    zero = jnp.zeros((8, LN), F32)
-
-    def clear(e, c):
-        for side in range(2):
-            for r in range(RC):
-                cs[e, r] = zero
-            for f in range(2):
-                rs[e, side, f] = jnp.zeros((DEPTH, ARCS), F32)
-        return c
-
-    lax.fori_loop(0, N_EX, clear, 0)
-    for e in range(2):
-        for r in range(XC):
-            ics[e, r] = zero
-
-    pl.semaphore_wait(barrier, NB - 1 + NH - 1)
-
     def to_blk(src, dst, send, recv):
         def go(k, c):
-            to = lax.rem(b + k, NB)
+            to = lax.rem(b + lax.rem(k + 14, NB - 1) + 1, NB)
             pltpu.make_async_remote_copy(
                 src_ref=src.at[to // 8], dst_ref=dst.at[b], send_sem=send.at[to],
                 recv_sem=recv.at[b], device_id=(to, ha), device_id_type=MESH,
@@ -258,18 +211,18 @@
         cols, rows = ics.at[e], irs.at[e]
         return halo(N_EX + e, (rows.at[0], rows.at[1]), irr.at[e], (cols, cols), icr.at[e])
 
-    def sweep(go, begin, end):
+    def sweep(go, begin, end, at_once=2):
         count = end - begin
 
-        def two(i, c):
-            go(begin + 2 * i)
-            go(begin + 2 * i + 1)
+        def some(i, c):
+            for j in range(at_once):
+                go(begin + at_once * i + j)
             return c
 
-        if count > 1:
-            lax.fori_loop(0, count // 2, two, 0)
-        if count % 2:
-            go(end - 1)
+        if count >= at_once:
+            lax.fori_loop(0, count // at_once, some, 0)
+        for j in range(count % at_once):
+            go(end - count % at_once + j)
 
     def start(copies):
         for copy in copies:
@@ -302,7 +255,7 @@
                 for i, half in enumerate(halves):
                     put_row(irs.at[e, side], m, x[i][k : k + 1], half)
 
-    def int_place(e, th):
+    def int_place(e):
         @pl.when(b == 0)
         def _():
             irr[e, 0] = irs[e, 0]
@@ -317,9 +270,7 @@
             own = pltpu.roll(ics[e, r], LN - 1, 1)
             low = jnp.where(at_low, own, icr[e, 0, r])
             high = jnp.where(at_high, own, pltpu.roll(icr[e, 1, r], LN - 2, 1))
-            icg[e, r] = jnp.where(odd, low, high)
-            th[0, r] = th[1, r]
-            th[NZ + 1, r] = th[NZ, r]
+            icg[e, r] = 0.15 * jnp.where(odd, low, high)
 
     def sides(x0, x1, ghost):
         a1, b1 = pltpu.roll(x0, 1, 1), pltpu.roll(x1, 1, 1)
@@ -328,23 +279,24 @@
         right = (jnp.where(final, b2, a2), jnp.where(final, ghost, b2))
         return left, right
 
-    def int_step(e, src, dst, last):
+    def int_step(src, dst, last):
+        for r in range(XC):
+            src[0, r] = src[1, r]
+            src[NZ + 1, r] = src[NZ, r]
+
         def go(m):
-            mine = pair == m
-            sums = [0.0, 0.0]
             for r in range(XC):
                 part = pl.ds(r, 8, stride=XC)
                 x = [src[m, r, :, half] for half in halves]
-                left, right = sides(x[0], x[1], pltpu.roll(icg[e, r], 129 - 2 * m, 1))
-                new = []
+                left, right = sides(x[0], x[1], 0.0)
                 for i, half in enumerate(halves):
                     t = x[i]
                     if r == 0:
-                        up = shift_rows(src[m, XC - 1, :, half], irr[e, 0, pl.ds(m - 1, 1), :][:, half], True)
+                        up = jnp.where(sub == 0, 0.0, pltpu.roll(src[m, XC - 1, :, half], 1, 0))
                     else:
                         up = src[m, r - 1, :, half]
                     if r == XC - 1:
-                        down = shift_rows(src[m, 0, :, half], irr[e, 1, pl.ds(m - 1, 1), :][:, half], False)
+                        down = jnp.where(sub == 7, 0.0, pltpu.roll(src[m, 0, :, half], 7, 0))
                     else:
                         down = src[m, r + 1, :, half]
                     total = (left[i] + right[i]) + (up + down) + (
@@ -353,23 +305,39 @@
                     alpha = al[m - 1, r, :, half] if last else xd[m - 1, i, part, :]
                     rate = jnp.exp2(C40 * (t * rcp(29.315 + t)))
                     rise = xa[m - 1, i, part, :] * (0.85 - alpha) * rate
-                    out = t + 0.15 * (total - 6.0 * t) + 4.0 * rise
                     if last:
                         xd[m - 1, i, part, :] = alpha + rise
-                        sums[i] = sums[i] + out
                     else:
                         al[m - 1, r, :, half] = alpha + rise
+                    dst[m, r, :, half] = t + 0.15 * (total - 6.0 * t) + 4.0 * rise
+
+        sweep(go, 1, NZ + 1, 4)
+
+    def int_fix(e, dst, last):
+        def go(m):
+            mine = pair == m
+            sums = [0.0, 0.0]
+            for r in range(XC):
+                ghost = pltpu.roll(icg[e, r], 129 - 2 * m, 1)
+                new = []
+                for i, half in enumerate(halves):
+                    out = dst[m, r, :, half] + jnp.where(final if i else first, ghost, 0.0)
+                    for side, at, k in ((0, 0, 0), (1, XC - 1, 7)):
+                        if r == at:
+                            row = jnp.broadcast_to(irr[e, side, pl.ds(m - 1, 1), :][:, half], (8, LN))
+                            out = out + jnp.where(sub == k, 0.15 * row, 0.0)
                     dst[m, r, :, half] = out
+                    sums[i] = sums[i] + out
                     new.append(out)
                 if not last:
                     int_pack(1, m, r, new, mine)
             if last:
                 for i, half in enumerate(halves):
-                    both = sums[i] + pltpu.roll(sums[i], 7, 0)
+                    pairs = sums[i] + pltpu.roll(sums[i], 7, 0)
                     for r in range(XC):
-                        put_row(csum.at[r], m, both[2 * r : 2 * r + 1], half)
-
-        sweep(go, 1, NZ + 1)
+                        put_row(csum.at[r], m, pairs[2 * r : 2 * r + 1], half)
+
+        sweep(go, 1, NZ + 1, 4)
 
     states = ((hb0, tb0, db0), (hb1, tb1, db1))
 
@@ -521,6 +489,9 @@
             gain = gain + (T[0, r] - T[1, r])
         ub[...] = gain
 
+    for e in range(2):
+        for r in range(XC):
+            ics[e, r] = zero
     wait(loads[0])
 
     def pack0(m, c):
@@ -533,8 +504,41 @@
         return c
 
     lax.fori_loop(1, NZ + 1, pack0, 0, unroll=2)
+    pl.semaphore_wait(barrier, NB - 1 + NH - 1)
     ex_i0 = int_halo(0)
     start(ex_i0)
+
+    col_load.wait()
+
+    col = col_ref[...]
+    owner = col >> 7
+    colf = jnp.broadcast_to(owner.astype(F32), (ARCS, ARCS))
+    owner_down = colf.T
+    q_i = lax.broadcasted_iota(jnp.int32, (ARCS, ARCS), 0)
+    p_i = lax.broadcasted_iota(jnp.int32, (ARCS, ARCS), 1)
+    earlier = jnp.where((owner_down == colf) & (q_i < p_i), 1.0, 0.0)
+    rank = jnp.sum(earlier, axis=0, keepdims=True).astype(jnp.int32)
+    ob = col >> 9
+    pos = (ob >> 3) * LN + (((ob + b) & 7) << 4) + ((owner & 3) << 2) + rank
+    posf = pos.astype(F32)
+    pos_down = jnp.broadcast_to(posf, (LN, ARCS)).T
+    val_down = jnp.broadcast_to((col & 511).astype(F32) + 1.0, (LN, ARCS)).T
+    lanes_a = lax.broadcasted_iota(jnp.int32, (ARCS, LN), 1).astype(F32)
+    for t in range(4):
+        hit = jnp.where(pos_down == lanes_a + float(t * LN), val_down, 0.0)
+        qs[t] = jnp.broadcast_to(jnp.sum(hit, axis=0, keepdims=True) - 1.0, (8, LN))
+    slot_i = lax.broadcasted_iota(jnp.int32, (4 * LN, ARCS), 0).astype(F32)
+    o2[...] = jnp.where(slot_i == posf, 1.0, 0.0).astype(BF16)
+
+    def clear(e, c):
+        for side in range(2):
+            for r in range(RC):
+                cs[e, r] = zero
+            for f in range(2):
+                rs[e, side, f] = jnp.zeros((DEPTH, ARCS), F32)
+        return c
+
+    lax.fori_loop(0, N_EX, clear, 0)
     to_blk(qs, qr, q_send, q_recv)
     for i in (1, 2, 3):
         wait(loads[i])
@@ -544,11 +548,13 @@
 
     wait(loads[4])
     wait(loads[5])
+    int_step(th0, th1, False)
     wait(ex_i0)
-    int_place(0, th0)
-    int_step(0, th0, th1, False)
+    int_place(0)
+    int_fix(0, th1, False)
     ex_i1 = int_halo(1)
     start(ex_i1)
+    int_step(th1, th0, True)
 
     wait(loads[6])
     wait(ex_s0)
@@ -558,10 +564,8 @@
     start(ex_b1)
 
     wait(ex_i1)
-    int_place(1, th1)
-    int_step(1, th1, th0, True)
-    store_deg = both(deg_out, xd, out_sem, 0, True)
-    start(store_deg)
+    int_place(1)
+    int_fix(1, th0, True)
     y_i = lax.broadcasted_iota(jnp.int32, (IY, LN), 0)
     c_i = lax.broadcasted_iota(jnp.int32, (IY, LN), 1)
 
@@ -648,10 +652,6 @@
     to_ha(ss, ubuf, u1_send, u1_recv)
 
     skin_step(3, 0, 4, None, WEDGE[3])
-    store_h = both(hum_out, xh, out_sem, 1, True)
-    store_t = both(stemp_out, xs, out_sem, 2, True)
-    start(store_h)
-    start(store_t)
 
     from_ha(ss, ubuf, u1_send, u1_recv)
     uptake = jnp.concatenate([ubuf[i] for i in range(NH)], axis=0)
@@ -669,10 +669,6 @@
         return c
 
     lax.fori_loop(1, NZ + 1, finish, 0, unroll=2)
-    store_th = both(temp_out, xt, out_sem, 3, True)
-    start(store_th)
-    for copies in (store_deg, store_h, store_t, store_th):
-        wait(copies)
 
 
 def on_device(int_temp, int_degree, int_affinity, hum, stemp, sdeg, ambient, colmap):
@@ -688,13 +684,16 @@
     outs = (interior, interior, skin, skin)
     msg = vmem((NB, 8, LN), F32)
     tiles = vmem((4, 8, LN), F32)
+    inside = pl.BlockSpec(memory_space=pltpu.VMEM)
+    int_half = jax.ShapeDtypeStruct((NZ, 2, IX, LN), F32)
+    skin_half = jax.ShapeDtypeStruct((DEPTH, 2, ROWS, LN), F32)
     results = pl.pallas_call(
         body,
-        out_shape=outs,
+        out_shape=(int_half, int_half, skin_half, skin_half),
         in_specs=[outside] * 8,
-        out_specs=(outside,) * 4,
+        out_specs=(inside,) * 4,
         scratch_shapes=[
-            int_stage, int_stage, int_stage, skin_stage, skin_stage, skin_stage,
+            int_stage, skin_stage,
             vmem((2, ROWS, LN), F32), vmem((1, ARCS), jnp.int32),
             int_buf, int_buf, vmem((NZ, XC, 8, IY), F32),
             skin_buf, skin_buf, skin_buf, skin_buf, skin_buf, skin_buf,
@@ -708,22 +707,25 @@
             vmem((XC, NZ, IY), F32), tiles, tiles, tiles, msg,
             vmem((8, ARCS), F32), tiles, msg, tiles, tiles,
             vmem((XC, NZ, IY), F32),
-            sem((15,)), sem((8,)), sem((N_EX + 2, 4)), sem((N_EX + 2, 4)),
+            sem((15,)), sem((N_EX + 2, 4)), sem((N_EX + 2, 4)),
             sem((NB,)), sem((NB,)), sem((NH,)), sem((NH,)),
             sem((NB,)), sem((NB,)), sem((NB,)), sem((NB,)), sem((NH,)), sem((NH,)),
         ],
         compiler_params=pltpu.CompilerParams(
-            collective_id=0, has_side_effects=True, vmem_limit_bytes=59 * 1024 * 1024
+            collective_id=0, has_side_effects=True, vmem_limit_bytes=50944 * 1024
         ),
         name="pylon",
-    )(int_temp, int_degree, int_affinity, hum, stemp, sdeg, ambient, colmap.reshape(1, ARCS))
+    )(*(
+        pltpu.with_memory_space_constraint(x, pltpu.HBM)
+        for x in (int_temp, int_degree, int_affinity, hum, stemp, sdeg, ambient, colmap.reshape(1, ARCS))
+    ))
     return pl.pallas_call(
         settle,
         out_shape=outs,
-        in_specs=[outside] * 4,
+        in_specs=[inside] * 4,
         out_specs=(outside,) * 4,
-        scratch_shapes=[vmem(x.shape, F32) for x in outs] + [sem((8,)), sem((8,))],
-        compiler_params=pltpu.CompilerParams(vmem_limit_bytes=59 * 1024 * 1024),
+        scratch_shapes=[sem((8,))],
+        compiler_params=pltpu.CompilerParams(vmem_limit_bytes=8 * 1024 * 1024),
         name="settle",
     )(*results)
 

time: 76 us -> 71.9 us (0.946)
  Pallas kernels: 75.2 us -> 71.1 us
    pallas_call x2, Pallas kernels: 75.2 us -> 71.1 us  [the longest x1 69 us: on_device(): pl.pallas_call(body, out_shape=(int_half, int_half, skin_half, skin_half)...]
where the time goes in v3:
time: 71.9 us; the launch traced here: 71.7 us
  Pallas kernels  71.1 us (99%)
    pallas_call x1, Pallas kernels, on_device(): pl.pallas_call(body, out_shape=(int_half, int_half, skin_half, skin_half)...  69 us
    pallas_call x1, Pallas kernels, on_device(): pl.pallas_call(settle, out_shape=outs, in_specs=[inside] * 4, out_specs=(...  2.07 us

profile of v3, /device:TPU:1, one launch (start us, length us, event | category | flops | bytes accessed | tf_op | source)
XLA Modules:
  0.0 71.7 jit_solution(6469566633156867364)
XLA Ops:
  0.6 69.0 %pylon.1 = (f32[32,2,32,128]{3,2,1,0:T(8,128)S(1)}, f32[32,2,32,128]{3,2,1,0:T(8,128)S(1)}, f32[16,2,64,128]{3,2,1,0:T(8,128)S(1)}, f32[16,2,64,128]{3,2,1,0:T(8,128)S(1)}) custom-call(f32[32,32,256]{2,1,0:T(8,128)} %temp_in.1, f32[32,32,256]{2,1,0:T(8,128)} %deg_in.1, f32[32,32,256]{2,1,0:T(8,128)} %aff_in.1, f32[16,64,256]{2,1,0:T(8,128)} %hum_in.1, ...), custom_call_target="tpu_custom_call" | custom-call | tf_op jit(solution)/shard_map/pylon/pallas_call | solution.py:690
  69.7 2.1 %settle.1 = (f32[32,32,256]{2,1,0:T(8,128)}, f32[32,32,256]{2,1,0:T(8,128)}, f32[16,64,256]{2,1,0:T(8,128)}, f32[16,64,256]{2,1,0:T(8,128)}) custom-call(f32[32,2,32,128]{3,2,1,0:T(8,128)S(1)} %get-tuple-element.8.refs_0_, f32[32,2,32,128]{3,2,1,0:T(8,128)S(1)} %get-tuple-element.9.refs_1_, f32[16,2,64,128]{3,2,1,0:T(8,128)S(1)} %get-tuple-element.10.refs_2_, ...), custom_call_target="tpu_custom_call" | custom-call | tf_op jit(solution)/shard_map/settle/pallas_call | solution.py:722

commit v4 on v3

--- a/solution.py
+++ b/solution.py
@@ -586,15 +586,14 @@
         row = lax.broadcasted_iota(jnp.int32, (4 * LN, LN), 0).astype(F32)
         oh[:, t * LN : (t + 1) * LN] = jnp.where(row == key, 1.0, 0.0).astype(BF16)
 
-    wait(ex_b1)
-    skin_place(1, BULK[1], False)
-
     from_ha(csend, abuf, x1_send, x1_recv)
     wide = pick(jnp.concatenate([abuf[i] for i in range(NH)], axis=1), oh[...])
     for t in range(4):
         ws[t] = wide[:, t * LN : (t + 1) * LN]
     to_blk(ws, rbuf, x2_send, x2_recv)
 
+    wait(ex_b1)
+    skin_place(1, BULK[1], False)
     skin_step(1, 2, DEPTH, BULK[2], BULK[1])
     ex_b2 = skin_halo(BULK[2])
     start(ex_b2)
@@ -625,10 +624,6 @@
     ex_w2 = skin_halo(WEDGE[2])
     start(ex_w2)
     inflow(2)
-
-    wait(ex_b3)
-    skin_place(3, BULK[3], False)
-    skin_step(3, 10, DEPTH, None, BULK[3])
 
     wait(ex_w2)
     skin_place(2, WEDGE[2], True)
@@ -641,7 +636,9 @@
         vs[t] = heat[:, t * LN : (t + 1) * LN]
     to_blk(vs, vr, u2_send, u2_recv)
 
-    skin_step(3, 4, 10, None, BULK[3])
+    wait(ex_b3)
+    skin_place(3, BULK[3], False)
+    skin_step(3, 4, DEPTH, None, BULK[3])
     wait(ex_w3)
     skin_place(3, WEDGE[3], True)
 

time: 71.9 us -> 71.3 us (level)
  no operation moved by 1% of the time
where the time goes in v4:
time: 71.3 us; the launch traced here: 71.2 us
  Pallas kernels  70.5 us (99%)
    pallas_call x1, Pallas kernels, on_device(): pl.pallas_call(body, out_shape=(int_half, int_half, skin_half, skin_half)...  68.4 us
    pallas_call x1, Pallas kernels, on_device(): pl.pallas_call(settle, out_shape=outs, in_specs=[inside] * 4, out_specs=(...  2.07 us

profile of v4, /device:TPU:1, one launch (start us, length us, event | category | flops | bytes accessed | tf_op | source)
XLA Modules:
  0.0 71.2 jit_solution(13048370593335705454)
XLA Ops:
  0.6 68.4 %pylon.1 = (f32[32,2,32,128]{3,2,1,0:T(8,128)S(1)}, f32[32,2,32,128]{3,2,1,0:T(8,128)S(1)}, f32[16,2,64,128]{3,2,1,0:T(8,128)S(1)}, f32[16,2,64,128]{3,2,1,0:T(8,128)S(1)}) custom-call(f32[32,32,256]{2,1,0:T(8,128)} %temp_in.1, f32[32,32,256]{2,1,0:T(8,128)} %deg_in.1, f32[32,32,256]{2,1,0:T(8,128)} %aff_in.1, f32[16,64,256]{2,1,0:T(8,128)} %hum_in.1, ...), custom_call_target="tpu_custom_call" | custom-call | tf_op jit(solution)/shard_map/pylon/pallas_call | solution.py:687
  69.1 2.1 %settle.1 = (f32[32,32,256]{2,1,0:T(8,128)}, f32[32,32,256]{2,1,0:T(8,128)}, f32[16,64,256]{2,1,0:T(8,128)}, f32[16,64,256]{2,1,0:T(8,128)}) custom-call(f32[32,2,32,128]{3,2,1,0:T(8,128)S(1)} %get-tuple-element.8.refs_0_, f32[32,2,32,128]{3,2,1,0:T(8,128)S(1)} %get-tuple-element.9.refs_1_, f32[16,2,64,128]{3,2,1,0:T(8,128)S(1)} %get-tuple-element.10.refs_2_, ...), custom_call_target="tpu_custom_call" | custom-call | tf_op jit(solution)/shard_map/settle/pallas_call | solution.py:719
